TPU v7x, 32 devices: a whole 2x2x4 slice. The times are simulated.
32 devices in a mesh: ctx: 8 (over z, y), head: 4 (over x, core).
Axes of the slice: x: 2, y: 2, z: 4, core: 2. Of those that a mesh axis runs over, the one named last changes fastest.
Arguments:
- queries: bfloat16 [4096, 4096], P('ctx', 'head'), may hold values from -160 to 160
- key_states: bfloat16 [4096, 4096], P('ctx', 'head'), may hold values from -160 to 160
- values: bfloat16 [4096, 4096], P('ctx', 'head'), may hold values from -6 to 6
- query_gain: bfloat16 [4096], P('head'), may hold values from 0.25 to 1.75
- key_gain: bfloat16 [4096], P('head'), may hold values from 0.25 to 1.75
- memory_blocks: int32 [8, 8], replicated, may hold values from 0 to 31, as said below
- cotangent: bfloat16 [4096, 4096], P('ctx', 'head'), may hold values from -6 to 6
Outputs:
- attended: bfloat16 [4096, 4096], P('ctx', 'head')
- query_grads: bfloat16 [4096, 4096], P('ctx', 'head')
- key_grads: bfloat16 [4096, 4096], P('ctx', 'head')
- value_grads: bfloat16 [4096, 4096], P('ctx', 'head')
Inputs may be any that keep to these rules, and one draw needn't show every extreme that they name: `memory_blocks`: row c lists the 8 blocks read by the tokens of ctx index c; block b holds tokens 128 b to 128 b + 127, and the 8 blocks of one row lie on 8 different ctx indices.
All inputs are finite; a program needn't handle non-finite values.
Results may differ from a plain program's by a relative error of at most 0.0045.
The roundings to bfloat16 on the way count: a program that leaves them out, or rounds other values in their place, can miss the bound.
Values may be sent and summed in bfloat16 or wider, within the bound.
A program may use at most 128 MiB of HBM per device.

v0:
```python
import math

import jax
import jax.numpy as jnp
from jax import lax
from jax.sharding import PartitionSpec as P

DH = 128
D = 4096
LEVELS = 4
BLOCK = 128


EPSILON = 1e-06
FLOOR_SCORE = -1e30


def from_partner(value, axis, bit):
    mask = 2**bit
    pairs = [(source, source ^ mask) for source in range(lax.axis_size(axis))]
    return lax.ppermute(value, axis, pairs)


def pick_rows(array, stride, offsets):
    shaped = array.reshape((array.shape[0] // stride, stride) + array.shape[1:])
    selector = jnp.arange(stride)[:, None] == offsets[None, :]
    selector = selector.reshape((1, stride, offsets.shape[0]) + (1,) * (array.ndim - 2))
    return jnp.sum(jnp.where(selector, shaped, jnp.zeros((), array.dtype)), axis=1)


def spread_rows(picked, stride, offsets, fill):
    selector = jnp.arange(stride)[:, None] == offsets[None, :]
    selector = selector.reshape((1, stride, offsets.shape[0]) + (1,) * (picked.ndim - 2))
    filled = jnp.where(selector, picked[:, None], jnp.asarray(fill, picked.dtype))
    return filled.reshape((picked.shape[0] * stride,) + picked.shape[1:])


def attend(query_rows, key_rows, value_rows, score_scale):
    scores = (
        jnp.einsum("qhd,khd->hqk", query_rows, key_rows, preferred_element_type=jnp.float32)
        * score_scale
    )
    row_max = jnp.max(scores, axis=2)
    weights = jnp.exp(scores - row_max[:, :, None])
    row_total = jnp.sum(weights, axis=2)
    summed = jnp.einsum(
        "hqk,khd->qhd", weights.astype(jnp.bfloat16), value_rows, preferred_element_type=jnp.float32
    )
    return (row_max.T, row_total.T, summed)


def attend_back(query_rows, key_rows, value_rows, grad_rows, log_sum, delta_rows, score_scale):
    scores = (
        jnp.einsum("qhd,khd->hqk", query_rows, key_rows, preferred_element_type=jnp.float32)
        * score_scale
    )
    softmax_rows = jnp.exp(scores - log_sum.T[:, :, None])
    grad_softmax = jnp.einsum(
        "qhd,khd->hqk", grad_rows, value_rows, preferred_element_type=jnp.float32
    )
    grad_scores = (softmax_rows * (grad_softmax - delta_rows.T[:, :, None])).astype(jnp.bfloat16)
    grad_query = (
        jnp.einsum("hqk,khd->qhd", grad_scores, key_rows, preferred_element_type=jnp.float32)
        * score_scale
    )
    grad_key = (
        jnp.einsum("hqk,qhd->khd", grad_scores, query_rows, preferred_element_type=jnp.float32)
        * score_scale
    )
    grad_value = jnp.einsum(
        "hqk,qhd->khd",
        softmax_rows.astype(jnp.bfloat16),
        grad_rows,
        preferred_element_type=jnp.float32,
    )
    return (grad_query, grad_key, grad_value)


def grow_level(key_pair, bit_total, ctx_index):
    for bit_index in range(bit_total):
        stacked = jnp.stack(key_pair)
        partner = from_partner(stacked, "ctx", bit_index)
        lower_side = ctx_index >> bit_index & 1 == 0
        joined = jnp.where(
            lower_side,
            jnp.concatenate([stacked, partner], 1),
            jnp.concatenate([partner, stacked], 1),
        )
        key_pair = (joined[0], joined[1])
    return key_pair


def shrink_level(grad_pair, bit_total, ctx_index):
    stacked = jnp.stack(grad_pair)
    for bit_index in reversed(range(bit_total)):
        half_rows = stacked.shape[1] // 2
        lower_part = stacked[:, :half_rows]
        upper_part = stacked[:, half_rows:]
        upper_side = ctx_index >> bit_index & 1 == 1
        outgoing = jnp.where(upper_side, lower_part, upper_part)
        retained = jnp.where(upper_side, upper_part, lower_part)
        stacked = retained + from_partner(outgoing.astype(jnp.bfloat16), "ctx", bit_index).astype(
            outgoing.dtype
        )
    return (stacked[0], stacked[1])


def shards(queries, key_states, values, query_gain, key_gain, memory_blocks, cotangent):
    row_count, feature_count = queries.shape
    heads_local = feature_count // DH
    score_scale = 1.0 / math.sqrt(DH)
    ctx_index = lax.axis_index("ctx")
    global_heads = lax.axis_index("head") * heads_local + jnp.arange(heads_local, dtype=jnp.int32)
    query_float = queries.astype(jnp.float32)
    key_float = key_states.astype(jnp.float32)
    query_squares, key_squares = lax.psum(
        (jnp.sum(query_float * query_float, axis=1), jnp.sum(key_float * key_float, axis=1)), "head"
    )
    query_inverse = lax.rsqrt(query_squares / D + EPSILON)[:, None]
    key_inverse = lax.rsqrt(key_squares / D + EPSILON)[:, None]
    query_normed = (
        (query_float * query_inverse * query_gain.astype(jnp.float32))
        .astype(jnp.bfloat16)
        .reshape(row_count, heads_local, DH)
    )
    key_normed = (
        (key_float * key_inverse * key_gain.astype(jnp.float32))
        .astype(jnp.bfloat16)
        .reshape(row_count, heads_local, DH)
    )
    value_rows = values.reshape(row_count, heads_local, DH)
    grad_rows = cotangent.reshape(row_count, heads_local, DH)
    level_keys = []
    for level_index in range(LEVELS):
        stride = 2**level_index
        offsets = global_heads % stride
        start_pair = (
            pick_rows(key_normed, stride, offsets),
            pick_rows(value_rows, stride, offsets),
        )
        level_keys.append(grow_level(start_pair, level_index, ctx_index))
    block_count = row_count // BLOCK
    reader_count = memory_blocks.shape[0]
    owner_table = memory_blocks // block_count
    local_table = memory_blocks % block_count
    wanted = jnp.sum(
        (owner_table == ctx_index)[:, :, None]
        & (local_table[:, :, None] == jnp.arange(block_count)[None, None, :]),
        axis=1,
    ).astype(jnp.bfloat16)
    own_list = lax.dynamic_index_in_dim(memory_blocks, ctx_index, 0, keepdims=False)
    chosen = ((own_list // block_count)[:, None] == jnp.arange(reader_count)[None, :]).astype(
        jnp.bfloat16
    )
    key_blocks = key_normed.reshape(block_count, BLOCK, heads_local, DH)
    value_blocks = value_rows.reshape(block_count, BLOCK, heads_local, DH)
    outgoing = jnp.stack(
        [
            jnp.einsum("rb,bthd->rthd", wanted, key_blocks, preferred_element_type=jnp.float32),
            jnp.einsum("rb,bthd->rthd", wanted, value_blocks, preferred_element_type=jnp.float32),
        ]
    ).astype(jnp.bfloat16)
    arrived = lax.all_to_all(outgoing, "ctx", split_axis=1, concat_axis=1, tiled=True)
    memory_keys = (
        jnp.einsum("jo,obhd->jbhd", chosen, arrived[0], preferred_element_type=jnp.float32)
        .astype(jnp.bfloat16)
        .reshape(-1, heads_local, DH)
    )
    memory_values = (
        jnp.einsum("jo,obhd->jbhd", chosen, arrived[1], preferred_element_type=jnp.float32)
        .astype(jnp.bfloat16)
        .reshape(-1, heads_local, DH)
    )
    part_max = []
    part_total = []
    part_sum = []
    for level_index in range(LEVELS):
        stride = 2**level_index
        offsets = global_heads % stride
        query_rows = pick_rows(query_normed, stride, offsets)
        row_max, row_total, summed = attend(
            query_rows, level_keys[level_index][0], level_keys[level_index][1], score_scale
        )
        part_max.append(spread_rows(row_max, stride, offsets, FLOOR_SCORE))
        part_total.append(spread_rows(row_total, stride, offsets, 0.0))
        part_sum.append(spread_rows(summed, stride, offsets, 0.0))
    row_max, row_total, summed = attend(query_normed, memory_keys, memory_values, score_scale)
    part_max.append(row_max)
    part_total.append(row_total)
    part_sum.append(summed)
    joint_max = jnp.max(jnp.stack(part_max), axis=0)
    joint_total = jnp.zeros_like(joint_max)
    numerator = jnp.zeros((row_count, heads_local, DH), jnp.float32)
    for part_index in range(len(part_max)):
        factor = jnp.exp(part_max[part_index] - joint_max)
        joint_total = joint_total + factor * part_total[part_index]
        numerator = numerator + factor[:, :, None] * part_sum[part_index]
    merged = numerator / joint_total[:, :, None]
    log_sum = joint_max + jnp.log(joint_total)
    delta_full = jnp.sum(grad_rows.astype(jnp.float32) * merged, axis=2)
    attended = merged.astype(jnp.bfloat16).reshape(row_count, feature_count)
    grad_query_normed = jnp.zeros((row_count, heads_local, DH), jnp.float32)
    level_grads = []
    for level_index in range(LEVELS):
        stride = 2**level_index
        offsets = global_heads % stride
        grad_query, grad_key, grad_value = attend_back(
            pick_rows(query_normed, stride, offsets),
            level_keys[level_index][0],
            level_keys[level_index][1],
            pick_rows(grad_rows, stride, offsets),
            pick_rows(log_sum, stride, offsets),
            pick_rows(delta_full, stride, offsets),
            score_scale,
        )
        grad_query_normed = grad_query_normed + spread_rows(grad_query, stride, offsets, 0.0)
        level_grads.append((grad_key, grad_value))
    grad_query, grad_key, grad_value = attend_back(
        query_normed, memory_keys, memory_values, grad_rows, log_sum, delta_full, score_scale
    )
    grad_query_normed = grad_query_normed + grad_query
    slot_grads = jnp.stack(
        [
            jnp.einsum(
                "jo,jbhd->obhd",
                chosen,
                grad_key.astype(jnp.bfloat16).reshape(-1, BLOCK, heads_local, DH),
                preferred_element_type=jnp.float32,
            ),
            jnp.einsum(
                "jo,jbhd->obhd",
                chosen,
                grad_value.astype(jnp.bfloat16).reshape(-1, BLOCK, heads_local, DH),
                preferred_element_type=jnp.float32,
            ),
        ]
    ).astype(jnp.bfloat16)
    returned = lax.all_to_all(slot_grads, "ctx", split_axis=1, concat_axis=1, tiled=True)
    grad_key_normed = jnp.einsum(
        "rb,rthd->bthd", wanted, returned[0], preferred_element_type=jnp.float32
    ).reshape(row_count, heads_local, DH)
    grad_value_total = jnp.einsum(
        "rb,rthd->bthd", wanted, returned[1], preferred_element_type=jnp.float32
    ).reshape(row_count, heads_local, DH)
    for level_index in range(LEVELS):
        stride = 2**level_index
        offsets = global_heads % stride
        own_key, own_value = shrink_level(level_grads[level_index], level_index, ctx_index)
        grad_key_normed = grad_key_normed + spread_rows(own_key, stride, offsets, 0.0)
        grad_value_total = grad_value_total + spread_rows(own_value, stride, offsets, 0.0)
    query_adjoint = query_gain.astype(jnp.float32) * grad_query_normed.reshape(
        row_count, feature_count
    )
    key_adjoint = key_gain.astype(jnp.float32) * grad_key_normed.reshape(row_count, feature_count)
    query_inner, key_inner = lax.psum(
        (jnp.sum(query_float * query_adjoint, axis=1), jnp.sum(key_float * key_adjoint, axis=1)),
        "head",
    )
    query_grads = (
        query_inverse * query_adjoint - query_float * query_inverse**3 * query_inner[:, None] / D
    ).astype(jnp.bfloat16)
    key_grads = (
        key_inverse * key_adjoint - key_float * key_inverse**3 * key_inner[:, None] / D
    ).astype(jnp.bfloat16)
    value_grads = grad_value_total.astype(jnp.bfloat16).reshape(row_count, feature_count)
    return (attended, query_grads, key_grads, value_grads)


def solution(mesh):
    in_specs = (
        P("ctx", "head"),
        P("ctx", "head"),
        P("ctx", "head"),
        P("head"),
        P("head"),
        P(),
        P("ctx", "head"),
    )
    out_specs = (P("ctx", "head"), P("ctx", "head"), P("ctx", "head"), P("ctx", "head"))
    return jax.shard_map(shards, mesh=mesh, in_specs=in_specs, out_specs=out_specs, check_vma=False)
```

profile of v0, /device:TPU:0, one launch (start us, length us, event | category | flops | bytes accessed | tf_op | source)
XLA Modules:
  0.0 493.2 jit_solution(10589930357507519047)
XLA Ops:
  4.0 8.3 %all-reduce.1 = (f32[512]{0:T(512)S(1)}, f32[512]{0:T(512)S(1)}) all-reduce(f32[512]{0:T(512)S(1)} %fusion.26, f32[512]{0:T(512)S(1)} %fusion.34), channel_id=1, replica_groups=mesh['ctx'=8,'head'=4] {'head'}, use_global_device_ids=true, to_apply=%region_1.0 | all-reduce | flops 1024 | bytes 8192 | tf_op jit(solution)/shard_map/psum | solution.py:116
  12.9 5.9 %select_reduce_fusion = (bf16[64,8,128]{2,1,0:T(8,128)(2,1)}, bf16[64,8,128]{2,1,0:T(8,128)(2,1)}, bf16[64,8,128]{2,1,0:T(8,128)(2,1)}, bf16[64,8,128]{2,1,0:T(8...) fusion(pred[8,8]{0,1:T(8,128)(4,1)S(1)} %iota_compare_fusion.2, bf16[512,1024]{1,0:T(8,128)(2,1)} %param.13, ...), kind=kLoop, calls=%fused_computation.183 | loop fusion | flops 8126464 | bytes 6828096 | tf_op jit(solution)/shard_map/reduce_sum | solution.py:28
  23.9 2.9 copy.286
  26.8 6.4 %all-to-all-start = ((bf16[2,8,128,8,128]{4,3,2,0,1:T(8,128)(2,1)}), bf16[2,8,128,8,128]{4,3,2,0,1:T(8,128)(2,1)}, u32[]{:S(2)}, u32[]{:S(2)}) async-start(bf16[2,8,128,8,128]{4,3,2,0,1:T(8,128)(2,1)} %copy.286), calls=%async_computation | async-start | bytes 8388608 | tf_op jit(solution)/shard_map/all_to_all | solution.py:163
  48.9 4.6 multiply_reduce_fusion.1
  67.0 51.6 %collective-permute-done.3 = bf16[2,64,8,128]{3,1,2,0:T(8,128)(2,1)} collective-permute-done((bf16[2,64,8,128]{3,1,2,0:T(8,128)(2,1)}, bf16[2,64,8,128]{3,1,2,0:T(8,128)(2,1)}, u32[]{:S(2)}, u32[]{:S(2)}) %collective-permute-start.3) | collective-permute-done | bytes 262176 | tf_op jit(solution)/shard_map/ppermute | solution.py:21
  121.3 5.4 %fusion.12 = f32[8,512]{1,0:T(8,128)} fusion(f32[8,512,512]{1,2,0:T(8,128)} %get-tuple-element.80, f32[8,512]{1,0:T(8,128)S(1)} %get-tuple-element.79), kind=kLoop, calls=%fused_computation.17 | loop fusion | flops 6287360 | bytes 8421376 | tf_op jit(solution)/shard_map/reduce_sum | solution.py:45
  126.8 2.6 maximum_select_fusion.3
  129.9 6.5 %collective-permute-done.4 = bf16[2,128,8,128]{3,1,2,0:T(8,128)(2,1)S(1)} collective-permute-done((bf16[2,128,8,128]{3,1,2,0:T(8,128)(2,1)S(1)}, bf16[2,128,8,128]{3,1,2,0:T(8,128)(2,1)S(1)}, u32[]{:S(2)}, u32[]{:S(2)}) %collective-permute-start.4) | collective-permute-done | bytes 524320 | tf_op jit(solution)/shard_map/ppermute | solution.py:21
  150.7 24.8 %collective-permute-done.2 = bf16[2,256,8,128]{3,1,2,0:T(8,128)(2,1)} collective-permute-done((bf16[2,256,8,128]{3,1,2,0:T(8,128)(2,1)}, bf16[2,256,8,128]{3,1,2,0:T(8,128)(2,1)}, u32[]{:S(2)}, u32[]{:S(2)}) %collective-permute-start.2) | collective-permute-done | bytes 1048608 | tf_op jit(solution)/shard_map/ppermute | solution.py:21
  175.6 2.8 maximum_select_fusion.1
  183.2 2.5 broadcast_in_dim.639
  185.7 3.1 copy.301
  191.2 2.8 maximum_select_fusion.2
  201.9 3.9 fusion.160
  207.6 3.0 copy.342
  210.6 4.1 multiply_reduce_fusion
  214.8 3.7 fusion.1
  224.3 6.8 %fusion.6 = f32[8,128,512]{2,1,0:T(8,128)} fusion(f32[8,512,1024]{2,1,0:T(8,128)S(1)} %get-tuple-element.72, f32[8,512]{1,0:T(8,128)S(1)} %get-tuple-element.71, bf16[1024,8,128]{2,1,0:T(8,128)(2,1)} %bitcast.434), kind=kOutput, calls=%fused_computation.9 | convolution fusion | flops 1086324736 | bytes 20987904 | tf_op jit(solution)/shard_map/hqk,khd->qhd/dot_general | solution.py:46
  231.1 9.9 %multiply_reduce_fusion.3 = (f32[512,8]{0,1:T(8,128)S(1)}, bf16[512,8,128]{0,2,1:T(8,128)(2,1)}) fusion(bf16[512,1024]{0,1:T(8,128)(2,1)S(1)} %copy-done.6, f32[512,8]{0,1:T(8,128)S(1)} %copy-done.110, f32[8,128,512]{2,1,0:T(8,128)} %fusion.6, f32[512,8]{0,1:T(8,128)S(1)} %copy-done.112, f32[512,8,128]{0,2,1:T(8,128)} %copy.303, ...), kind=kOutput, calls=%fused_computation.129 | convolution fusion | flops 552071168 | bytes 20066304 | tf_op jit(solution)/shard_map/hqk,khd->qhd/dot_general | solution.py:46
  247.1 4.7 fusion.86
  257.0 9.2 %fusion.78 = bf16[8,1024,128]{2,1,0:T(8,128)(2,1)} fusion(bf16[512,8,128]{0,2,1:T(8,128)(2,1)S(1)} %bitcast.431, f32[8,512,1024]{2,1,0:T(8,128)} %copy-done, f32[8,512]{1,0:T(8,128)S(1)} %bitcast.495), kind=kOutput, calls=%fused_computation.138 | convolution fusion | flops 1087373312 | bytes 19939328 | tf_op jit(solution)/shard_map/hqk,qhd->khd/dot_general | solution.py:70
  266.2 9.5 %fusion = bf16[8,512,1024]{2,1,0:T(8,128)(2,1)S(1)} fusion(f32[8,512,1024]{2,1,0:T(8,128)} %copy-done, bf16[512,8,128]{0,2,1:T(8,128)(2,1)} %bitcast.430, f32[8,512]{1,0:T(8,128)S(1)} %bitcast.501, f32[8,512]{1,0:T(8,128)S(1)} %bitcast.496, bf16[1024,8,128]{2,1,0:T(8,128)(2,1)} %bitcast.435), kind=kOutput, calls=%fused_computation.1 | convolution fusion | flops 1094713344 | bytes 28344320 | tf_op jit(solution)/shard_map/qhd,khd->hqk/dot_general | solution.py:58
  279.6 3.3 copy.345
  287.3 2.8 copy.349
  290.1 4.9 %all-to-all-start.1 = ((bf16[2,8,128,8,128]{4,3,2,0,1:T(8,128)(2,1)}), bf16[2,8,128,8,128]{4,3,2,0,1:T(8,128)(2,1)}, u32[]{:S(2)}, u32[]{:S(2)}) async-start(bf16[2,8,128,8,128]{4,3,2,0,1:T(8,128)(2,1)} %copy.349), calls=%async_computation.1 | async-start | bytes 8388608 | tf_op jit(solution)/shard_map/all_to_all | solution.py:238
  295.1 3.6 select_convert_fusion.2
  317.7 2.5 copy.326
  320.2 2.7 broadcast_in_dim.652
  322.9 3.0 copy.327
  325.9 2.8 fusion.97
  330.7 2.5 broadcast_in_dim.655
  333.3 3.0 copy.335
  339.3 3.1 copy.338
  342.4 4.6 multiply_convert_fusion
  349.1 10.9 %bitcast_add_fusion.2 = f32[512,8,128]{0,2,1:T(8,128)} fusion(f32[512,8,128]{0,2,1:T(8,128)} %copy.338, f32[512,8,128]{0,2,1:T(8,128)} %copy.335, f32[512,8,128]{0,2,1:T(8,128)} %copy.327, f32[8,128,512]{2,1,0:T(8,128)} %fusion.163, bf16[1024,8,128]{0,2,1:T(8,128)(2,1)} %copy.342, bf16[8,512,1024]{2,1,0:T(8,128)(2,1)} %copy-done.3, ...), kind=kOutput, calls=%fused_computation.102 | convolution fusion | flops 1078460416 | bytes 20983808 | tf_op jit(solution)/shard_map/hqk,khd->qhd/dot_general | solution.py:63
  360.1 3.1 fusion.15
  366.4 2.9 copy.370
  371.3 2.5 copy.377
  378.8 2.5 copy.357
  382.6 51.0 %collective-permute-done.9 = bf16[2,256,8,128]{1,3,2,0:T(8,128)(2,1)} collective-permute-done((bf16[2,256,8,128]{1,3,2,0:T(8,128)(2,1)}, bf16[2,256,8,128]{1,3,2,0:T(8,128)(2,1)}, u32[]{:S(2)}, u32[]{:S(2)}) %collective-permute-start.9) | collective-permute-done | bytes 1048608 | tf_op jit(solution)/shard_map/ppermute | solution.py:21
  433.6 3.0 convert_add_fusion
  440.7 9.1 %collective-permute-done.10 = bf16[2,128,8,128]{1,3,2,0:T(8,128)(2,1)S(1)} collective-permute-done((bf16[2,128,8,128]{1,3,2,0:T(8,128)(2,1)S(1)}, bf16[2,128,8,128]{1,3,2,0:T(8,128)(2,1)S(1)}, u32[]{:S(2)}, u32[]{:S(2)}) %collective-permute-start.10) | collective-permute-done | bytes 524320 | tf_op jit(solution)/shard_map/ppermute | solution.py:21
  457.8 5.8 %collective-permute-done.11 = bf16[2,64,8,128]{1,3,2,0:T(8,128)(2,1)} collective-permute-done((bf16[2,64,8,128]{1,3,2,0:T(8,128)(2,1)}, bf16[2,64,8,128]{1,3,2,0:T(8,128)(2,1)}, u32[]{:S(2)}, u32[]{:S(2)}) %collective-permute-start.11) | collective-permute-done | bytes 262176 | tf_op jit(solution)/shard_map/ppermute | solution.py:21
  466.2 2.5 fusion.159
  476.9 6.0 %fusion.41 = (f32[512]{0:T(512)S(1)}, f32[512,1024]{1,0:T(8,128)}, bf16[512,1024]{1,0:T(8,128)(2,1)}) fusion(bf16[512,1024]{1,0:T(8,128)(2,1)S(1)} %copy-done.24, pred[512,1024]{1,0:T(8,128)(4,1)S(1)} %copy-done.64, f32[64,8,128]{2,1,0:T(8,128)S(1)} %copy.365, pred[512,1024]{1,0:T(8,128)(4,1)S(1)} %copy-done.63, f32[64,8,8,128]{3,2,1,0:T(8,128)S(1)} %bitcast.453, ...), kind=kLoop, calls=%fused_computation.66 | loop fusion | flops 9960960 | bytes 23074816 | tf_op jit(solution)/shard_map/reduce_sum | solution.py:256
  482.9 5.6 %all-reduce = (f32[512]{0:T(512)S(1)}, f32[512]{0:T(512)S(1)}) all-reduce(f32[512]{0:T(512)S(1)} %fusion.33, f32[512]{0:T(512)S(1)} %get-tuple-element.42), channel_id=1, replica_groups=mesh['ctx'=8,'head'=4] {'head'}, use_global_device_ids=true, to_apply=%region_35.36 | all-reduce | flops 1024 | bytes 8192 | tf_op jit(solution)/shard_map/psum | solution.py:255
  488.5 2.9 fusion.32
  (442 shorter events, 158.9 us)
Async XLA Ops:
  0.6 12.3 %copy-start.25 = (bf16[512,1024]{1,0:T(8,128)(2,1)S(1)}, bf16[512,1024]{1,0:T(8,128)(2,1)}, u32[]{:S(2)}) copy-start(bf16[512,1024]{1,0:T(8,128)(2,1)} %param.7) | copy-start | bytes 3145732
  0.6 12.3 %copy-start.23 = (bf16[512,1024]{1,0:T(8,128)(2,1)S(1)}, bf16[512,1024]{1,0:T(8,128)(2,1)}, u32[]{:S(2)}) copy-start(bf16[512,1024]{1,0:T(8,128)(2,1)} %param.8) | copy-start | bytes 3145732
  3.9 14.9 %copy-start.117 = (pred[8,8]{0,1:T(8,128)(4,1)}, pred[8,8]{0,1:T(8,128)(4,1)S(1)}, u32[]{:S(2)}) copy-start(pred[8,8]{0,1:T(8,128)(4,1)S(1)} %iota_compare_fusion.2) | copy-start | bytes 196
  3.9 14.9 %copy-start.99 = (f32[1024]{0:T(1024)}, f32[1024]{0:T(1024)S(1)}, u32[]{:S(2)}) copy-start(f32[1024]{0:T(1024)S(1)} %convert_element_type.197) | copy-start | bytes 12292
  4.0 14.9 %copy-start.101 = (f32[1024]{0:T(1024)}, f32[1024]{0:T(1024)S(1)}, u32[]{:S(2)}) copy-start(f32[1024]{0:T(1024)S(1)} %convert_element_type.200) | copy-start | bytes 12292
  12.9 5.9 %copy-start.106 = (f32[512]{0:T(512)}, f32[512]{0:T(512)S(1)}, u32[]{:S(2)}) copy-start(f32[512]{0:T(512)S(1)} %get-tuple-element.68) | copy-start | bytes 6148
  12.9 5.9 %copy-start.108 = (f32[512]{0:T(512)}, f32[512]{0:T(512)S(1)}, u32[]{:S(2)}) copy-start(f32[512]{0:T(512)S(1)} %get-tuple-element.84) | copy-start | bytes 6148
  18.9 14.3 %copy-start.35 = (bf16[512,1024]{1,0:T(8,128)(2,1)}, bf16[512,1024]{1,0:T(8,128)(2,1)S(1)}, u32[]{:S(2)}) copy-start(bf16[512,1024]{1,0:T(8,128)(2,1)S(1)} %get-tuple-element.50) | copy-start | bytes 3145732
  26.8 175.1 %all-to-all-start = ((bf16[2,8,128,8,128]{4,3,2,0,1:T(8,128)(2,1)}), bf16[2,8,128,8,128]{4,3,2,0,1:T(8,128)(2,1)}, u32[]{:S(2)}, u32[]{:S(2)}) async-start(bf16[2,8,128,8,128]{4,3,2,0,1:T(8,128)(2,1)} %copy.286), calls=%async_computation | async-start | bytes 8388608 | tf_op jit(solution)/shard_map/all_to_all | solution.py:163
  39.1 99.2 %collective-permute-start = (bf16[2,256,8,128]{3,1,2,0:T(8,128)(2,1)}, bf16[2,256,8,128]{3,1,2,0:T(8,128)(2,1)}, u32[]{:S(2)}, u32[]{:S(2)}) collective-permute-start(bf16[2,256,8,128]{3,1,2,0:T(8,128)(2,1)} %pad_maximum_fusion.5), channel_id=1, source_target_pairs={{0,4},{4,0},{8,12},{12,8},{16,20},{20,16},{24,28},{28,24},{1,5},{5... | collective-permute-start | bytes 3145736 | tf_op jit(solution)/shard_map/ppermute | solution.py:21
  44.8 81.9 %collective-permute-start.1 = (bf16[2,128,8,128]{3,1,2,0:T(8,128)(2,1)}, bf16[2,128,8,128]{3,1,2,0:T(8,128)(2,1)}, u32[]{:S(2)}, u32[]{:S(2)}) collective-permute-start(bf16[2,128,8,128]{3,1,2,0:T(8,128)(2,1)} %pad_maximum_fusion.6), channel_id=1, source_target_pairs={{0,4},{4,0},{8,12},{12,8},{16,20},{20,16},{24,28},{28,24},{1,5},{5... | collective-permute-start | bytes 1572872 | tf_op jit(solution)/shard_map/ppermute | solution.py:21
  45.8 72.8 %collective-permute-start.3 = (bf16[2,64,8,128]{3,1,2,0:T(8,128)(2,1)}, bf16[2,64,8,128]{3,1,2,0:T(8,128)(2,1)}, u32[]{:S(2)}, u32[]{:S(2)}) collective-permute-start(bf16[2,64,8,128]{3,1,2,0:T(8,128)(2,1)} %pad_maximum_fusion.7), channel_id=1, source_target_pairs={{0,4},{4,0},{8,12},{12,8},{16,20},{20,16},{24,28},{28,24},{1,5},{5... | collective-permute-start | bytes 786440 | tf_op jit(solution)/shard_map/ppermute | solution.py:21
  53.5 67.8 %copy-start.81 = (f32[8,512]{1,0:T(8,128)}, f32[8,512]{1,0:T(8,128)S(1)}, u32[]{:S(2)}) copy-start(f32[8,512]{1,0:T(8,128)S(1)} %get-tuple-element.79) | copy-start | bytes 49156
  56.2 83.9 %copy-start.48 = (bf16[256,8,128]{0,2,1:T(8,128)(2,1)}, bf16[256,8,128]{0,2,1:T(8,128)(2,1)S(1)}, u32[]{:S(2)}) copy-start(bf16[256,8,128]{0,2,1:T(8,128)(2,1)S(1)} %copy.355) | copy-start | bytes 1572868
  60.7 57.9 %copy-start.69 = (bf16[64,8,128]{2,0,1:T(8,128)(2,1)S(1)}, bf16[64,8,128]{2,0,1:T(8,128)(2,1)}, u32[]{:S(2)}) copy-start(bf16[64,8,128]{2,0,1:T(8,128)(2,1)} %copy-done.68) | copy-start | bytes 393220
  119.8 16.6 %collective-permute-start.4 = (bf16[2,128,8,128]{3,1,2,0:T(8,128)(2,1)S(1)}, bf16[2,128,8,128]{3,1,2,0:T(8,128)(2,1)S(1)}, u32[]{:S(2)}, u32[]{:S(2)}) collective-permute-start(bf16[2,128,8,128]{3,1,2,0:T(8,128)(2,1)S(1)} %maximum_select_fusion.5), channel_id=1, source_target_pairs={{0,8},{4,12},{8,0},{12,4},{16,24},{20,28},{24,16},{28,20},{1,9},{5... | collective-permute-start | bytes 1572872 | tf_op jit(solution)/shard_map/ppermute | solution.py:21
  126.7 11.5 %copy-start.44 = (bf16[256,8,128]{2,0,1:T(8,128)(2,1)S(1)}, bf16[256,8,128]{2,0,1:T(8,128)(2,1)}, u32[]{:S(2)}) copy-start(bf16[256,8,128]{2,0,1:T(8,128)(2,1)} %copy-done.43) | copy-start | bytes 1572868
  126.7 11.5 %copy-start.46 = (bf16[256,8,128]{2,0,1:T(8,128)(2,1)S(1)}, bf16[256,8,128]{2,0,1:T(8,128)(2,1)}, u32[]{:S(2)}) copy-start(bf16[256,8,128]{2,0,1:T(8,128)(2,1)} %copy-done.45) | copy-start | bytes 1572868
  129.3 46.2 %collective-permute-start.2 = (bf16[2,256,8,128]{3,1,2,0:T(8,128)(2,1)}, bf16[2,256,8,128]{3,1,2,0:T(8,128)(2,1)}, u32[]{:S(2)}, u32[]{:S(2)}) collective-permute-start(bf16[2,256,8,128]{3,1,2,0:T(8,128)(2,1)} %maximum_select_fusion.3), channel_id=1, source_target_pairs={{0,8},{4,12},{8,0},{12,4},{16,24},{20,28},{24,16},{28,20},{1,9},{5... | collective-permute-start | bytes 3145736 | tf_op jit(solution)/shard_map/ppermute | solution.py:21
  137.7 53.5 %collective-permute-start.5 = (bf16[2,256,8,128]{3,1,2,0:T(8,128)(2,1)}, bf16[2,256,8,128]{3,1,2,0:T(8,128)(2,1)}, u32[]{:S(2)}, u32[]{:S(2)}) collective-permute-start(bf16[2,256,8,128]{3,1,2,0:T(8,128)(2,1)} %maximum_select_fusion.4), channel_id=1, source_target_pairs={{0,16},{4,20},{8,24},{12,28},{16,0},{20,4},{24,8},{28,12},{1,17},{... | collective-permute-start | bytes 3145736 | tf_op jit(solution)/shard_map/ppermute | solution.py:21
  150.7 27.6 %copy-start.60 = (bf16[128,8,128]{0,2,1:T(8,128)(2,1)S(1)}, bf16[128,8,128]{0,2,1:T(8,128)(2,1)}, u32[]{:S(2)}) copy-start(bf16[128,8,128]{0,2,1:T(8,128)(2,1)} %copy.359) | copy-start | bytes 786436
  178.9 10.0 %copy-start.4 = (f32[8,128,512]{2,1,0:T(8,128)}, f32[8,128,512]{2,1,0:T(8,128)S(1)}, u32[]{:S(2)}) copy-start(f32[8,128,512]{2,1,0:T(8,128)S(1)} %get-tuple-element.76) | copy-start | bytes 6291460
  214.7 9.6 %copy-start = (f32[8,512,1024]{2,1,0:T(8,128)}, f32[8,512,1024]{2,1,0:T(8,128)S(1)}, u32[]{:S(2)}) copy-start(f32[8,512,1024]{2,1,0:T(8,128)S(1)} %get-tuple-element.72) | copy-start | bytes 50331652
  214.8 5.9 %copy-start.41 = (bf16[1,8,128,8,128]{4,3,2,0,1:T(8,128)(2,1)S(1)}, bf16[1,8,128,8,128]{4,3,2,0,1:T(8,128)(2,1)}, u32[]{:S(2)}) copy-start(bf16[1,8,128,8,128]{4,3,2,0,1:T(8,128)(2,1)} %get-tuple-element.53) | copy-start | bytes 6291460
  214.8 5.9 %copy-start.121 = (s32[8]{0:T(128)S(1)}, s32[8]{0:T(128)}, u32[]{:S(2)}) copy-start(s32[8]{0:T(128)} %and_select_fusion) | copy-start | bytes 100
  224.3 6.8 %copy-start.6 = (bf16[512,1024]{0,1:T(8,128)(2,1)S(1)}, bf16[512,1024]{0,1:T(8,128)(2,1)}, u32[]{:S(2)}) copy-start(bf16[512,1024]{0,1:T(8,128)(2,1)} %copy.314) | copy-start | bytes 3145732
  224.3 6.8 %copy-start.110 = (f32[512,8]{0,1:T(8,128)S(1)}, f32[512,8]{0,1:T(8,128)}, u32[]{:S(2)}) copy-start(f32[512,8]{0,1:T(8,128)} %get-tuple-element.45) | copy-start | bytes 49156
  224.3 6.8 %copy-start.111 = (f32[512,8]{0,1:T(8,128)S(1)}, f32[512,8]{0,1:T(8,128)}, u32[]{:S(2)}) copy-start(f32[512,8]{0,1:T(8,128)} %get-tuple-element.46) | copy-start | bytes 49156
  224.3 6.8 %copy-start.112 = (f32[512,8]{0,1:T(8,128)S(1)}, f32[512,8]{0,1:T(8,128)}, u32[]{:S(2)}) copy-start(f32[512,8]{0,1:T(8,128)} %get-tuple-element.47) | copy-start | bytes 49156
  224.3 6.8 %copy-start.114 = (f32[512,8]{0,1:T(8,128)S(1)}, f32[512,8]{0,1:T(8,128)}, u32[]{:S(2)}) copy-start(f32[512,8]{0,1:T(8,128)} %get-tuple-element.64) | copy-start | bytes 49156
  224.3 6.8 %copy-start.115 = (f32[512,8]{0,1:T(8,128)S(1)}, f32[512,8]{0,1:T(8,128)}, u32[]{:S(2)}) copy-start(f32[512,8]{0,1:T(8,128)} %get-tuple-element.65) | copy-start | bytes 49156
  231.1 12.7 %copy-start.126 = (pred[2,8]{1,0:T(4,128)(4,1)S(1)}, pred[2,8]{1,0:T(4,128)(4,1)}, u32[]{:S(2)}) copy-start(pred[2,8]{1,0:T(4,128)(4,1)} %copy-done.125) | copy-start | bytes 52
  241.0 10.8 %copy-start.78 = (f32[512,8]{0,1:T(8,128)}, f32[512,8]{0,1:T(8,128)S(1)}, u32[]{:S(2)}) copy-start(f32[512,8]{0,1:T(8,128)S(1)} %get-tuple-element.57) | copy-start | bytes 49156
  241.0 6.1 %copy-start.50 = (bf16[256,8,128]{0,2,1:T(8,128)(2,1)S(1)}, bf16[256,8,128]{0,2,1:T(8,128)(2,1)}, u32[]{:S(2)}) copy-start(bf16[256,8,128]{0,2,1:T(8,128)(2,1)} %copy.356) | copy-start | bytes 1572868
  241.2 10.6 %copy-start.57 = (f32[512,8]{1,0:T(8,128)}, f32[512,8]{1,0:T(8,128)S(1)}, u32[]{:S(2)}) copy-start(f32[512,8]{1,0:T(8,128)S(1)} %copy.323) | copy-start | bytes 49156
  257.0 9.2 %copy-start.79 = (f32[512,8]{0,1:T(8,128)S(1)}, f32[512,8]{0,1:T(8,128)}, u32[]{:S(2)}) copy-start(f32[512,8]{0,1:T(8,128)} %copy-done.78) | copy-start | bytes 49156
  290.1 176.0 %all-to-all-start.1 = ((bf16[2,8,128,8,128]{4,3,2,0,1:T(8,128)(2,1)}), bf16[2,8,128,8,128]{4,3,2,0,1:T(8,128)(2,1)}, u32[]{:S(2)}, u32[]{:S(2)}) async-start(bf16[2,8,128,8,128]{4,3,2,0,1:T(8,128)(2,1)} %copy.349), calls=%async_computation.1 | async-start | bytes 8388608 | tf_op jit(solution)/shard_map/all_to_all | solution.py:238
  295.1 9.6 %copy-start.5 = (f32[8,128,512]{2,1,0:T(8,128)S(1)}, f32[8,128,512]{2,1,0:T(8,128)}, u32[]{:S(2)}) copy-start(f32[8,128,512]{2,1,0:T(8,128)} %copy-done.4) | copy-start | bytes 6291460
  298.7 75.5 %collective-permute-start.6 = (bf16[2,256,8,128]{1,3,2,0:T(8,128)(2,1)}, bf16[2,256,8,128]{1,3,2,0:T(8,128)(2,1)}, u32[]{:S(2)}, u32[]{:S(2)}) collective-permute-start(bf16[2,256,8,128]{1,3,2,0:T(8,128)(2,1)} %select_convert_fusion.2), channel_id=1, source_target_pairs={{0,4},{4,0},{8,12},{12,8},{16,20},{20,16},{24,28},{28,24},{1,5},{5... | collective-permute-start | bytes 3145736 | tf_op jit(solution)/shard_map/ppermute | solution.py:21
  309.4 127.4 %collective-permute-start.7 = (bf16[2,256,8,128]{1,3,2,0:T(8,128)(2,1)}, bf16[2,256,8,128]{1,3,2,0:T(8,128)(2,1)}, u32[]{:S(2)}, u32[]{:S(2)}) collective-permute-start(bf16[2,256,8,128]{1,3,2,0:T(8,128)(2,1)} %select_convert_fusion.1), channel_id=1, source_target_pairs={{0,8},{4,12},{8,0},{12,4},{16,24},{20,28},{24,16},{28,20},{1,9},{5... | collective-permute-start | bytes 3145736 | tf_op jit(solution)/shard_map/ppermute | solution.py:21
  315.3 118.3 %collective-permute-start.9 = (bf16[2,256,8,128]{1,3,2,0:T(8,128)(2,1)}, bf16[2,256,8,128]{1,3,2,0:T(8,128)(2,1)}, u32[]{:S(2)}, u32[]{:S(2)}) collective-permute-start(bf16[2,256,8,128]{1,3,2,0:T(8,128)(2,1)} %select_convert_fusion), channel_id=1, source_target_pairs={{0,16},{4,20},{8,24},{12,28},{16,0},{20,4},{24,8},{28,12},{1,17},{... | collective-permute-start | bytes 3145736 | tf_op jit(solution)/shard_map/ppermute | solution.py:21
  347.0 13.0 %slice-start = ((s8[8388608]{0:T(1024)(128)(4,1)}), s8[4194304]{0:T(1024)(128)(4,1)S(1)}, s32[]{:S(2)}) async-start(s8[8388608]{0:T(1024)(128)(4,1)} %bitcast.424), calls=%async_computation.2 | async-start | bytes 8388608
  349.1 10.9 %slice-start.1 = ((s8[8388608]{0:T(1024)(128)(4,1)}), s8[4194304]{0:T(1024)(128)(4,1)S(1)}, s32[]{:S(2)}) async-start(s8[8388608]{0:T(1024)(128)(4,1)} %bitcast.424), calls=%async_computation.3 | async-start | bytes 8388608
  436.8 13.1 %collective-permute-start.10 = (bf16[2,128,8,128]{1,3,2,0:T(8,128)(2,1)S(1)}, bf16[2,128,8,128]{1,3,2,0:T(8,128)(2,1)S(1)}, u32[]{:S(2)}, u32[]{:S(2)}) collective-permute-start(bf16[2,128,8,128]{1,3,2,0:T(8,128)(2,1)S(1)} %select_convert_fusion.4), channel_id=1, source_target_pairs={{0,8},{4,12},{8,0},{12,4},{16,24},{20,28},{24,16},{28,20},{1,9},{5... | collective-permute-start | bytes 1572872 | tf_op jit(solution)/shard_map/ppermute | solution.py:21
  439.2 13.3 %collective-permute-start.8 = (bf16[2,128,8,128]{1,3,2,0:T(8,128)(2,1)S(1)}, bf16[2,128,8,128]{1,3,2,0:T(8,128)(2,1)S(1)}, u32[]{:S(2)}, u32[]{:S(2)}) collective-permute-start(bf16[2,128,8,128]{1,3,2,0:T(8,128)(2,1)S(1)} %select_convert_fusion.5), channel_id=1, source_target_pairs={{0,4},{4,0},{8,12},{12,8},{16,20},{20,16},{24,28},{28,24},{1,5},{5... | collective-permute-start | bytes 1572872 | tf_op jit(solution)/shard_map/ppermute | solution.py:21
  451.0 12.6 %collective-permute-start.11 = (bf16[2,64,8,128]{1,3,2,0:T(8,128)(2,1)}, bf16[2,64,8,128]{1,3,2,0:T(8,128)(2,1)}, u32[]{:S(2)}, u32[]{:S(2)}) collective-permute-start(bf16[2,64,8,128]{1,3,2,0:T(8,128)(2,1)} %select_convert_fusion.3), channel_id=1, source_target_pairs={{0,4},{4,0},{8,12},{12,8},{16,20},{20,16},{24,28},{28,24},{1,5},{5... | collective-permute-start | bytes 786440 | tf_op jit(solution)/shard_map/ppermute | solution.py:21
  476.9 11.7 %copy-start.109 = (f32[512]{0:T(512)S(1)}, f32[512]{0:T(512)}, u32[]{:S(2)}) copy-start(f32[512]{0:T(512)} %copy-done.108) | copy-start | bytes 6148
  476.9 11.7 %copy-start.124 = (f32[512]{0:T(512)S(1)}, f32[512]{0:T(512)}, u32[]{:S(2)}) copy-start(f32[512]{0:T(512)} %get-tuple-element.85) | copy-start | bytes 6148
  (99 other events, 278.4 us)
where the time goes:
time: 500 us; the launch traced here: 493 us
  waiting for transfers between devices  149 us (30%)
  local copies, waits for them, and re-layouts  121 us (24%)
  matrix products  104 us (21%)
  other arithmetic  75.3 us (15%)
  starting transfers between devices  26.9 us (5%)
  blocking collectives  14 us (3%)
    ppermute x12, waiting for transfers between devices, from_partner(): return lax.ppermute(value, axis, pairs)  149 us
    broadcast_in_dim x44, local copies, waits for them, and re-layouts, spread_rows(): jnp.where(selector, picked[:, None], jnp.asarray(fill, picked.dtype))  45.4 us
    unnamed x273, local copies, waits for them, and re-layouts  22.9 us
    dot_general x5, matrix products, attend(): jnp.einsum('hqk,khd->qhd', weights.astype(jnp.bfloat16), value_rows, pref...  21.3 us
    dot_general x5, matrix products, attend_back(): jnp.einsum('hqk,khd->qhd', grad_scores, key_rows, preferred_element_type=...  19 us
    dot_general x5, matrix products, attend_back(): jnp.einsum('hqk,qhd->khd', softmax_rows.astype(jnp.bfloat16), grad_rows,...  18.7 us
    dot_general x5, matrix products, attend_back(): jnp.einsum('qhd,khd->hqk', grad_rows, value_rows, preferred_element_type=...  16.8 us
    ppermute x12, starting transfers between devices, from_partner(): return lax.ppermute(value, axis, pairs)  15.6 us
  transfers between devices with their start and end apart: 14, of which 6 were waited for; matrix products, arithmetic and copies ran while one was open for 33% of the time, Pallas kernels for 0%

commit v1 on v0

v1 whole, which is shorter than its diff:
```python
import functools
import math

import jax
import jax.numpy as jnp
import numpy as np
from jax import lax
from jax.experimental import pallas as pl
from jax.experimental.pallas import tpu as pltpu
from jax.sharding import PartitionSpec as P

DH = 128
D = 4096
LEVELS = 4
BLOCK = 128


EPSILON = 1e-06
FLOOR_SCORE = -1e30


SEG = 512
CLASSES = 8
PER = SEG // CLASSES
ORDER = (0, 4, 2, 6, 1, 3, 5, 7)
SCALE = 1.0 / math.sqrt(DH)
EXP2_SCALE = SCALE * math.log2(math.e)
VMEM_BYTES = 56 * 2**20


def dot_nt(left, right):
    return lax.dot_general(left, right, (((1,), (1,)), ((), ())), preferred_element_type=jnp.float32)


def dot_nn(left, right):
    return lax.dot_general(left, right, (((1,), (0,)), ((), ())), preferred_element_type=jnp.float32)


def dot_tn(left, right):
    return lax.dot_general(left, right, (((0,), (0,)), ((), ())), preferred_element_type=jnp.float32)


def class_matrix():
    matrix = np.zeros((SEG, SEG), np.float32)
    for residue in range(CLASSES):
        for index in range(PER):
            matrix[residue * PER + index, index * CLASSES + residue] = 1.0
    return jnp.asarray(matrix, jnp.bfloat16)


def class_rows(first_head, head, residue):
    start = (first_head + head + residue) % CLASSES * PER
    return pl.ds(start if isinstance(start, int) else pl.multiple_of(start, PER), PER)


def first_class(heads):
    return 0 if heads % CLASSES == 0 else lax.axis_index("head") * heads % CLASSES


def split_kernel(matrix_ref, rows_ref, heads_ref, sorted_ref):
    heads = heads_ref.shape[0]
    first_head = first_class(heads)
    sorted_ref[...] = dot_nn(matrix_ref[...], rows_ref[...]).astype(jnp.bfloat16)
    for head in range(heads):
        for place, residue in enumerate(ORDER):
            heads_ref[head, place * PER : (place + 1) * PER, :] = sorted_ref[
                class_rows(first_head, head, residue), head * DH : (head + 1) * DH
            ]


def join_kernel(matrix_ref, heads_ref, rows_ref, sorted_ref):
    heads = heads_ref.shape[0]
    first_head = first_class(heads)
    for head in range(heads):
        for place, residue in enumerate(ORDER):
            sorted_ref[class_rows(first_head, head, residue), head * DH : (head + 1) * DH] = heads_ref[
                head, place * PER : (place + 1) * PER, :
            ]
    rows_ref[...] = dot_tn(matrix_ref[...], sorted_ref[...]).astype(jnp.bfloat16)


def vmem_call(kernel, outs, scratch=(), operand_count=0, smem_first=False, flops=0):
    specs = [pl.BlockSpec(memory_space=pltpu.VMEM)] * operand_count
    if smem_first:
        specs = [pl.BlockSpec(memory_space=pltpu.SMEM)] + specs[1:]
    return pl.pallas_call(
        kernel,
        out_shape=outs,
        in_specs=specs,
        out_specs=jax.tree.map(lambda _: pl.BlockSpec(memory_space=pltpu.VMEM), outs),
        scratch_shapes=list(scratch),
        cost_estimate=pl.CostEstimate(flops=flops, bytes_accessed=2**23, transcendentals=flops // 512),
        compiler_params=pltpu.CompilerParams(vmem_limit_bytes=VMEM_BYTES),
    )


def split_heads(matrix, rows):
    width = rows.shape[1]
    out = jax.ShapeDtypeStruct((width // DH, SEG, DH), jnp.bfloat16)
    scratch = [pltpu.VMEM((SEG, width), jnp.bfloat16)]
    return vmem_call(split_kernel, out, scratch, operand_count=2, flops=2 * SEG * SEG * width)(matrix, rows)


def join_heads(matrix, heads):
    width = heads.shape[0] * DH
    out = jax.ShapeDtypeStruct((SEG, width), jnp.bfloat16)
    scratch = [pltpu.VMEM((SEG, width), jnp.bfloat16)]
    return vmem_call(join_kernel, out, scratch, operand_count=2, flops=2 * SEG * SEG * width)(matrix, heads)


def take_block(ref, block):
    seg, local = block // (SEG // BLOCK), block % (SEG // BLOCK)
    piece = BLOCK // CLASSES
    rows = ref[seg, :, pl.ds(pl.multiple_of(local * piece, piece), piece), :]
    return rows.reshape(BLOCK, DH)


def add_block(ref, block, term):
    seg, local = block // (SEG // BLOCK), block % (SEG // BLOCK)
    piece = BLOCK // CLASSES
    place = (seg, slice(None), pl.ds(pl.multiple_of(local * piece, piece), piece), slice(None))
    ref[place] = ref[place] + term.reshape(CLASSES, piece, DH)


def take_rows(ref, segs, classes):
    return jnp.concatenate([ref[seg, :classes].reshape(classes * PER, DH) for seg in segs], axis=0)


def take_lanes(ref, segs, count):
    return jnp.concatenate([ref[seg, :, :count] for seg in segs], axis=1)


def part_forward(query_rows, key_rows, value_rows):
    scores = dot_nt(key_rows, query_rows)
    row_max = jnp.max(scores, axis=0, keepdims=True) * EXP2_SCALE
    weights = jnp.exp2(scores * EXP2_SCALE - row_max)
    total = jnp.sum(weights, axis=0, keepdims=True)
    return row_max, total, dot_tn(value_rows, weights.astype(jnp.bfloat16))


def merge_parts(parts):
    joint = functools.reduce(jnp.maximum, [part[0] for part in parts])
    factors = [jnp.exp2(part[0] - joint) for part in parts]
    total = sum(factor * part[1] for factor, part in zip(factors, parts))
    summed = sum(factor * part[2] for factor, part in zip(factors, parts))
    return joint, total, summed


def forward_kernel(
    slots, blocks_ref, query_ref, key_ref, value_ref, query_r_ref, key_r_ref, query_gain_ref, key_gain_ref,
    out_ref, merged_ref, lse_ref, qn_ref, kn_ref, max_ref, total_ref,
):
    segs = query_ref.shape[0]

    def normalise(seg, carry):
        for raw, inverse, gain, normed in (
            (query_ref, query_r_ref, query_gain_ref, qn_ref),
            (key_ref, key_r_ref, key_gain_ref, kn_ref),
        ):
            rows = raw[seg].reshape(SEG, DH).astype(jnp.float32) * inverse[seg] * gain[...]
            normed[seg] = rows.astype(jnp.bfloat16).reshape(CLASSES, PER, DH)
        return carry

    lax.fori_loop(0, segs, normalise, 0)

    def own_and_memory(seg, carry):
        query_rows = take_rows(qn_ref, [seg], CLASSES)
        own = part_forward(query_rows, take_rows(kn_ref, [seg], CLASSES), take_rows(value_ref, [seg], CLASSES))
        listed = [blocks_ref[seg, slot] for slot in range(slots)]
        memory = part_forward(
            query_rows,
            jnp.concatenate([take_block(kn_ref, block) for block in listed], axis=0),
            jnp.concatenate([take_block(value_ref, block) for block in listed], axis=0),
        )
        max_ref[seg], total_ref[seg], merged_ref[seg] = merge_parts([own, memory])
        return carry

    lax.fori_loop(0, segs, own_and_memory, 0)

    def fold(members, count, parts):
        old = (
            take_lanes(max_ref, members, count),
            take_lanes(total_ref, members, count),
            take_lanes(merged_ref, members, count),
        )
        joint, total, summed = merge_parts([old] + parts)
        for place, seg in enumerate(members):
            lanes = slice(place * count, (place + 1) * count)
            max_ref[seg, :, :count] = joint[:, lanes]
            total_ref[seg, :, :count] = total[:, lanes]
            merged_ref[seg, :, :count] = summed[:, lanes]

    def level_one(group, carry):
        members = [2 * group, 2 * group + 1]
        part = part_forward(*(take_rows(ref, members, 4) for ref in (qn_ref, kn_ref, value_ref)))
        fold(members, 4 * PER, [part])
        return carry

    lax.fori_loop(0, segs // 2, level_one, 0)

    def upper_levels(group, carry):
        members = [4 * group + place for place in range(4)]
        key_members = [group // 2 * 8 + place for place in range(8)]
        query_rows, key_rows, value_rows = (take_rows(ref, members, 2) for ref in (qn_ref, kn_ref, value_ref))
        second = part_forward(query_rows, key_rows, value_rows)
        third_max, third_total, third_sum = part_forward(
            query_rows, take_rows(kn_ref, key_members, 1), take_rows(value_ref, key_members, 1)
        )
        inside = lax.broadcasted_iota(jnp.int32, third_max.shape, 1) % (2 * PER) < PER
        third_max = jnp.where(inside, third_max, FLOOR_SCORE)
        fold(members, 2 * PER, [second, (third_max, third_total, third_sum)])
        return carry

    lax.fori_loop(0, segs // 4, upper_levels, 0)

    def finish(seg, carry):
        total = total_ref[seg]
        merged = merged_ref[seg] / total
        merged_ref[seg] = merged
        lse_ref[seg] = max_ref[seg] + jnp.log2(total)
        out_ref[seg] = merged.T.astype(jnp.bfloat16)
        return carry

    lax.fori_loop(0, segs, finish, 0)


def part_backward(query_rows, key_rows, value_rows, grad_rows, lse, delta):
    softmax_rows = jnp.exp2(dot_nt(key_rows, query_rows) * EXP2_SCALE - lse)
    grad_scores = (softmax_rows * (dot_nt(value_rows, grad_rows) - delta)).astype(jnp.bfloat16)
    return (
        dot_tn(key_rows, grad_scores) * SCALE,
        dot_nn(grad_scores, query_rows) * SCALE,
        dot_nn(softmax_rows.astype(jnp.bfloat16), grad_rows),
    )


def backward_kernel(
    slots, blocks_ref, qn_ref, kn_ref, value_ref, grad_ref, merged_ref, lse_ref,
    dq_ref, dk_ref, dv_ref, delta_ref, dqt_ref, dvf_ref,
):
    segs = qn_ref.shape[0]
    own_refs = (qn_ref, kn_ref, value_ref, grad_ref)

    def own_level(seg, carry):
        grad_float = grad_ref[seg].reshape(SEG, DH).astype(jnp.float32)
        delta = jnp.sum(grad_float.T * merged_ref[seg], axis=0, keepdims=True)
        delta_ref[seg] = delta
        dqt, dk, dv = part_backward(*(take_rows(ref, [seg], CLASSES) for ref in own_refs), lse_ref[seg], delta)
        dqt_ref[seg] = dqt
        dk_ref[seg] = dk.reshape(CLASSES, PER, DH)
        dvf_ref[seg] = dv.reshape(CLASSES, PER, DH)
        return carry

    lax.fori_loop(0, segs, own_level, 0)

    def memory(seg, carry):
        query_rows = take_rows(qn_ref, [seg], CLASSES)
        grad_rows = take_rows(grad_ref, [seg], CLASSES)
        for first in range(0, slots, 4):
            listed = [blocks_ref[seg, slot] for slot in range(first, min(first + 4, slots))]
            dqt, dk, dv = part_backward(
                query_rows,
                jnp.concatenate([take_block(kn_ref, block) for block in listed], axis=0),
                jnp.concatenate([take_block(value_ref, block) for block in listed], axis=0),
                grad_rows, lse_ref[seg], delta_ref[seg],
            )
            dqt_ref[seg] = dqt_ref[seg] + dqt
            dk = dk.astype(jnp.bfloat16).astype(jnp.float32)
            dv = dv.astype(jnp.bfloat16).astype(jnp.float32)
            for place, block in enumerate(listed):
                rows = slice(place * BLOCK, (place + 1) * BLOCK)
                add_block(dk_ref, block, dk[rows])
                add_block(dvf_ref, block, dv[rows])
        return carry

    lax.fori_loop(0, segs, memory, 0)

    def spread(members, classes, key_members, key_classes, grads):
        dqt, dk, dv = grads
        count = classes * PER
        for place, seg in enumerate(members):
            dqt_ref[seg, :, :count] = dqt_ref[seg, :, :count] + dqt[:, place * count : (place + 1) * count]
        count = key_classes * PER
        for place, seg in enumerate(key_members):
            rows = slice(place * count, (place + 1) * count)
            shape = (key_classes, PER, DH)
            dk_ref[seg, :key_classes] = dk_ref[seg, :key_classes] + dk[rows].reshape(shape)
            dvf_ref[seg, :key_classes] = dvf_ref[seg, :key_classes] + dv[rows].reshape(shape)

    def level_one(group, carry):
        members = [2 * group, 2 * group + 1]
        grads = part_backward(
            *(take_rows(ref, members, 4) for ref in own_refs),
            take_lanes(lse_ref, members, 4 * PER), take_lanes(delta_ref, members, 4 * PER),
        )
        spread(members, 4, members, 4, grads)
        return carry

    lax.fori_loop(0, segs // 2, level_one, 0)

    def upper_levels(group, carry):
        members = [4 * group + place for place in range(4)]
        key_members = [group // 2 * 8 + place for place in range(8)]
        query_rows, key_rows, value_rows, grad_rows = (take_rows(ref, members, 2) for ref in own_refs)
        lse = take_lanes(lse_ref, members, 2 * PER)
        delta = take_lanes(delta_ref, members, 2 * PER)
        spread(members, 2, members, 2, part_backward(query_rows, key_rows, value_rows, grad_rows, lse, delta))
        inside = lax.broadcasted_iota(jnp.int32, lse.shape, 1) % (2 * PER) < PER
        third = part_backward(
            query_rows, take_rows(kn_ref, key_members, 1), take_rows(value_ref, key_members, 1),
            grad_rows, jnp.where(inside, lse, -FLOOR_SCORE), delta,
        )
        spread(members, 2, key_members, 1, third)
        return carry

    lax.fori_loop(0, segs // 4, upper_levels, 0)

    def finish(seg, carry):
        dq_ref[seg] = dqt_ref[seg].T
        dv_ref[seg] = dvf_ref[seg].reshape(SEG, DH).astype(jnp.bfloat16)
        return carry

    lax.fori_loop(0, segs, finish, 0)


def to_head_order(vector, head):
    parts = vector.reshape(-1, PER, CLASSES)
    rolled = lax.dynamic_slice_in_dim(jnp.concatenate([parts, parts], axis=2), head, CLASSES, axis=2)
    return jnp.stack([rolled[:, :, residue] for residue in ORDER], axis=1).reshape(vector.shape)


def from_head_order(vector, head):
    parts = vector.reshape(-1, CLASSES, PER)
    natural = jnp.stack([parts[:, ORDER.index(residue)] for residue in range(CLASSES)], axis=2)
    doubled = jnp.concatenate([natural, natural], axis=2)
    return lax.dynamic_slice_in_dim(doubled, (CLASSES - head) % CLASSES, CLASSES, axis=2).reshape(vector.shape)


def exchange(heads):
    return lax.all_to_all(heads, "ctx", split_axis=0, concat_axis=0, tiled=True)


def send_heads(heads):
    return exchange(jnp.concatenate([heads] * (lax.axis_size("ctx") // heads.shape[0]), axis=0))


def head_shards(queries, key_states, values, query_gain, key_gain, memory_blocks, cotangent):
    segs, slots = memory_blocks.shape
    heads_local = queries.shape[1] // DH
    local_head = lax.axis_index("ctx") % heads_local
    head = (lax.axis_index("head") * heads_local + local_head) % CLASSES
    matrix = class_matrix()
    query_heads = send_heads(split_heads(matrix, queries))
    key_heads = send_heads(split_heads(matrix, key_states))
    value_heads = send_heads(split_heads(matrix, values))
    grad_heads = send_heads(split_heads(matrix, cotangent))
    squares = jnp.stack(
        [jnp.sum(jnp.square(rows.astype(jnp.float32)), axis=1) for rows in (queries, key_states)]
    )
    squares = lax.psum(squares, "head")
    squares = lax.all_gather(squares, "ctx", axis=1)
    inverse = lax.rsqrt(squares / D + EPSILON)
    inverse = jnp.stack([to_head_order(inverse[0], head), to_head_order(inverse[1], head)])
    gains = [
        lax.dynamic_slice_in_dim(gain, local_head * DH, DH).astype(jnp.float32)[None, :]
        for gain in (query_gain, key_gain)
    ]
    classed = (segs, CLASSES, PER, DH)
    flat = (segs, SEG, DH)
    shape = jax.ShapeDtypeStruct
    pairs = segs * SEG * SEG * 4
    attended, merged, lse, query_normed, key_normed = vmem_call(
        functools.partial(forward_kernel, slots),
        (
            shape(flat, jnp.bfloat16), shape((segs, DH, SEG), jnp.float32), shape((segs, 1, SEG), jnp.float32),
            shape(classed, jnp.bfloat16), shape(classed, jnp.bfloat16),
        ),
        [pltpu.VMEM((segs, 1, SEG), jnp.float32)] * 2,
        operand_count=8, smem_first=True, flops=pairs * DH * 4,
    )(
        memory_blocks, query_heads.reshape(classed), key_heads.reshape(classed), value_heads.reshape(classed),
        inverse[0][:, :, None], inverse[1][:, :, None], *gains,
    )
    attended = exchange(attended)
    dq, dk, dv = vmem_call(
        functools.partial(backward_kernel, slots),
        (shape(flat, jnp.float32), shape(classed, jnp.float32), shape(flat, jnp.bfloat16)),
        [
            pltpu.VMEM((segs, 1, SEG), jnp.float32), pltpu.VMEM((segs, DH, SEG), jnp.float32),
            pltpu.VMEM(classed, jnp.float32),
        ],
        operand_count=7, smem_first=True, flops=pairs * DH * 10,
    )(
        memory_blocks, query_normed, key_normed, value_heads.reshape(classed), grad_heads.reshape(classed),
        merged, lse,
    )
    value_grads = exchange(dv)
    raw = [query_heads.astype(jnp.float32), key_heads.astype(jnp.float32)]
    adjoint = [gains[0] * dq, gains[1] * dk.reshape(flat)]
    inner = jnp.stack([from_head_order(jnp.sum(raw[i] * adjoint[i], axis=2), head) for i in range(2)])
    if segs > heads_local:
        inner = jnp.where(lax.axis_index("ctx") < heads_local, inner, 0.0)
    inner = lax.psum(inner, ("ctx", "head"))
    grads = []
    for i in range(2):
        scale = inverse[i][:, :, None]
        weight = inverse[i] ** 3 * to_head_order(inner[i], head) / D
        grads.append(exchange((scale * adjoint[i] - raw[i] * weight[:, :, None]).astype(jnp.bfloat16)))
    return tuple(join_heads(matrix, heads[:heads_local]) for heads in (attended, grads[0], grads[1], value_grads))


def solution(mesh):
    in_specs = (
        P("ctx", "head"),
        P("ctx", "head"),
        P("ctx", "head"),
        P("head"),
        P("head"),
        P(),
        P("ctx", "head"),
    )
    out_specs = (P("ctx", "head"), P("ctx", "head"), P("ctx", "head"), P("ctx", "head"))
    return jax.shard_map(head_shards, mesh=mesh, in_specs=in_specs, out_specs=out_specs, check_vma=False)
```

time: 500 us -> 345 us (0.69); the launches traced: 493 us -> 344 us
  matrix products: 104 us -> 0 us
  local copies, waits for them, and re-layouts: 121 us -> 19.5 us
  Pallas kernels: 0 us -> 86.6 us
  blocking collectives: 14 us -> 86.5 us
  other arithmetic: 75.3 us -> 12.8 us
  waiting for transfers between devices: 149 us -> 99.5 us
  starting transfers between devices: 26.9 us -> 37.5 us
    ppermute x12 -> x0, waiting for transfers between devices: 149 us -> none  [from_partner(): return lax.ppermute(value, axis, pairs)]
    dot_general x38 -> x0, matrix products: 104 us -> none  [the longest x5 21.3 us: attend(): jnp.einsum('hqk,khd->qhd', weights.astype(jnp.bfloat16), value_rows, pref...]
    all_to_all x2 -> x8, waiting for transfers between devices: 0.01 us -> 99.5 us  [exchange(): return lax.all_to_all(heads, 'ctx', split_axis=0, concat_axis=0, tiled=True)]
    pallas_call x0 -> x10, Pallas kernels: none -> 86.6 us  [the longest x1 34.1 us: head_shards(): vmem_call(functools.partial(backward_kernel, slots), (shape(flat, jnp.flo...]
    broadcast_in_dim x50 -> x0, local copies, waits for them, and re-layouts: 50.5 us -> none  [the longest x44 45.4 us: spread_rows(): jnp.where(selector, picked[:, None], jnp.asarray(fill, picked.dtype))]
    all_gather x0 -> x1, blocking collectives: none -> 38.8 us  [head_shards(): squares = lax.all_gather(squares, 'ctx', axis=1)]
    psum x2, blocking collectives: 14 us -> 47.7 us  [the longest x1 40.9 us: head_shards(): inner = lax.psum(inner, ('ctx', 'head'))]
    reduce_sum x16 -> x4, other arithmetic: 35.1 us -> 5.07 us  [the longest x2 4.51 us: head_shards(): jnp.sum(raw[i] * adjoint[i], axis=2)]
  transfers between devices with their start and end apart: 14 -> 8, of which waited for: 6 -> 5; matrix products, arithmetic and copies ran while one was open for 33% -> 9% of each run, Pallas kernels for 0% -> 23%
where the time goes in v1:
time: 345 us; the launch traced here: 344 us
  waiting for transfers between devices  99.5 us (29%)
  Pallas kernels  86.6 us (25%)
  blocking collectives  86.5 us (25%)
  starting transfers between devices  37.5 us (11%)
  local copies, waits for them, and re-layouts  19.5 us (6%)
  other arithmetic  12.8 us (4%)
    all_to_all x8, waiting for transfers between devices, exchange(): return lax.all_to_all(heads, 'ctx', split_axis=0, concat_axis=0, tiled=True)  99.5 us
    psum x1, blocking collectives, head_shards(): inner = lax.psum(inner, ('ctx', 'head'))  40.9 us
    all_gather x1, blocking collectives, head_shards(): squares = lax.all_gather(squares, 'ctx', axis=1)  38.8 us
    all_to_all x8, starting transfers between devices, exchange(): return lax.all_to_all(heads, 'ctx', split_axis=0, concat_axis=0, tiled=True)  37.5 us
    pallas_call x1, Pallas kernels, head_shards(): vmem_call(functools.partial(backward_kernel, slots), (shape(flat, jnp.flo...  34.1 us
    pallas_call x1, Pallas kernels, head_shards(): vmem_call(functools.partial(forward_kernel, slots), (shape(flat, jnp.bflo...  27 us
    pallas_call x4, Pallas kernels, split_heads(): vmem_call(split_kernel, out, scratch, operand_count=2, flops=2 * SEG * SE...  12.8 us
    pallas_call x4, Pallas kernels, join_heads(): vmem_call(join_kernel, out, scratch, operand_count=2, flops=2 * SEG * SEG...  12.6 us
  transfers between devices with their start and end apart: 8, of which 5 were waited for; matrix products, arithmetic and copies ran while one was open for 9% of the time, Pallas kernels for 23%

profile of v1, /device:TPU:0, one launch (start us, length us, event | category | flops | bytes accessed | tf_op | source)
XLA Modules:
  0.0 343.7 jit_solution(17882040846935487478)
XLA Ops:
  0.6 3.2 shard_map.113
  3.8 7.4 %all-to-all-start.2 = ((bf16[8,512,128]{2,1,0:T(8,128)(2,1)}), bf16[8,512,128]{2,1,0:T(8,128)(2,1)S(1)}, u32[]{:S(2)}, u32[]{:S(2)}) async-start(bf16[8,512,128]{2,1,0:T(8,128)(2,1)} %shard_map.113), calls=%async_computation.2 | async-start | bytes 2097152 | tf_op jit(solution)/shard_map/all_to_all | solution.py:340
  11.2 3.2 shard_map.111
  14.7 22.3 %all-to-all-done.2 = bf16[8,512,128]{2,1,0:T(8,128)(2,1)S(1)} async-done(((bf16[8,512,128]{2,1,0:T(8,128)(2,1)}), bf16[8,512,128]{2,1,0:T(8,128)(2,1)S(1)}, u32[]{:S(2)}, u32[]{:S(2)}) %all-to-all-start.2) | async-done | bytes 1048608 | tf_op jit(solution)/shard_map/all_to_all | solution.py:340
  37.0 1.0 copy-done.10
  38.0 3.6 %all-to-all-start = ((bf16[8,512,128]{2,1,0:T(8,128)(2,1)}), bf16[8,512,128]{2,1,0:T(8,128)(2,1)S(1)}, u32[]{:S(2)}, u32[]{:S(2)}) async-start(bf16[8,512,128]{2,1,0:T(8,128)(2,1)} %shard_map.111), calls=%async_computation | async-start | bytes 2097152 | tf_op jit(solution)/shard_map/all_to_all | solution.py:340
  41.9 6.8 %psum.14 = f32[2,1,512]{2,0,1:T(2,128)S(1)} all-reduce(f32[2,1,512]{2,0,1:T(2,128)S(1)} %maximum_bitcast_fusion), channel_id=1, replica_groups=mesh['ctx'=8,'head'=4] {'head'}, use_global_device_ids=true, to_apply=%region_2.3 | all-reduce | flops 1024 | bytes 8192 | tf_op jit(solution)/shard_map/psum | solution.py:360
  48.6 38.8 %all_gather.7 = f32[2,8,512]{2,0,1:T(2,128)S(1)} all-gather(f32[2,1,512]{2,0,1:T(2,128)S(1)} %psum.14), channel_id=1, replica_groups=mesh['ctx'=8,'head'=4] {'ctx'}, dimensions={1}, use_global_device_ids=true | all-gather | bytes 36864 | tf_op jit(solution)/shard_map/all_gather | solution.py:361
  87.9 3.2 shard_map.112
  91.5 1.1 slice_reduce_fusion.16
  92.6 1.1 slice_reduce_fusion.24
  93.8 3.6 %all-to-all-start.1 = ((bf16[8,512,128]{2,1,0:T(8,128)(2,1)}), bf16[8,512,128]{2,1,0:T(8,128)(2,1)S(1)}, u32[]{:S(2)}, u32[]{:S(2)}) async-start(bf16[8,512,128]{2,1,0:T(8,128)(2,1)} %shard_map.112), calls=%async_computation.1 | async-start | bytes 2097152 | tf_op jit(solution)/shard_map/all_to_all | solution.py:340
  97.4 3.3 shard_map.116
  100.8 17.4 %all-to-all-done.1 = bf16[8,512,128]{2,1,0:T(8,128)(2,1)S(1)} async-done(((bf16[8,512,128]{2,1,0:T(8,128)(2,1)}), bf16[8,512,128]{2,1,0:T(8,128)(2,1)S(1)}, u32[]{:S(2)}, u32[]{:S(2)}) %all-to-all-start.1) | async-done | bytes 1048608 | tf_op jit(solution)/shard_map/all_to_all | solution.py:340
  118.2 3.7 %all-to-all-start.4 = ((bf16[8,512,128]{2,1,0:T(8,128)(2,1)}), bf16[8,512,128]{2,1,0:T(8,128)(2,1)S(1)}, u32[]{:S(2)}, u32[]{:S(2)}) async-start(bf16[8,512,128]{2,1,0:T(8,128)(2,1)} %shard_map.116), calls=%async_computation.4 | async-start | bytes 2097152 | tf_op jit(solution)/shard_map/all_to_all | solution.py:340
  122.1 3.4 broadcast_in_dim_squeeze_stack_reshape.10.query_r_ref
  125.6 3.4 broadcast_in_dim_squeeze_stack_reshape.11.key_r_ref
  129.1 0.6 fusion.14.query_gain_ref
  129.8 0.7 fusion.13.key_gain_ref
  130.4 27.0 %shard_map.114 = (bf16[8,512,128]{2,1,0:T(8,128)(2,1)}, f32[8,128,512]{2,1,0:T(8,128)}, f32[8,1,512]{2,1,0:T(1,128)}, bf16[8,8,64,128]{3,2,1,0:T(8,128)(2,1)}, bf16[8,8,64,128]{3,2,1,0:T(8,128)(2,1)}) custom-call(s32[8,8]{1,0:T(8,128)} %blocks_ref.3, bf16[8,8,64,128]{3,2,1,0:T(8,128)(2,1)} %bitcast.122, bf16[8,8,64,128]{3,2,1,0:T(8,128)(2,1)} %bitcast.123, ...), custom_call_target="tpu_custom_call" | custom-call | flops 4294967296 | bytes 8388608 | tf_op jit(solution)/shard_map/pallas_call | solution.py:372
  157.5 5.7 %all-to-all-start.3 = ((bf16[8,512,128]{2,1,0:T(8,128)(2,1)}), bf16[8,512,128]{2,1,0:T(8,128)(2,1)S(1)}, u32[]{:S(2)}, u32[]{:S(2)}) async-start(bf16[8,512,128]{2,1,0:T(8,128)(2,1)} %get-tuple-element.12), calls=%async_computation.3 | async-start | bytes 2097152 | tf_op jit(solution)/shard_map/all_to_all | solution.py:340
  163.2 34.1 %shard_map.117 = (f32[8,512,128]{2,1,0:T(8,128)}, f32[8,8,64,128]{3,2,1,0:T(8,128)}, bf16[8,512,128]{2,1,0:T(8,128)(2,1)}) custom-call(s32[8,8]{1,0:T(8,128)} %blocks_ref.3, bf16[8,8,64,128]{3,2,1,0:T(8,128)(2,1)} %get-tuple-element.13.qn_ref, bf16[8,8,64,128]{3,2,1,0:T(8,128)(2,1)} %get-tuple-element.14.kn_ref, bf16[8,8,64,128]{3,2,1,0:T(8,128)(2,1)} %bitcast.125, ...), custom_call_target="tpu_custom_call" | custom-call | flops 10737418240 | bytes 8388608 | tf_op jit(solution)/shard_map/pallas_call | solution.py:385
  197.3 2.3 fusion
  199.7 2.2 fusion.3
  202.4 0.4 copy-done.12
  203.1 0.6 constant_dynamic-update-slice_fusion.33
  203.7 0.6 constant_dynamic-update-slice_fusion.32
  204.3 0.8 constant_dynamic-slice_fusion
  205.4 40.9 %psum.15 = f32[2,8,512]{2,1,0:T(8,128)S(1)} all-reduce(f32[2,8,512]{2,1,0:T(8,128)S(1)} %pad_maximum_fusion), channel_id=1, replica_groups=mesh['ctx'=8,'head'=4] {'ctx','head'}, use_global_device_ids=true, to_apply=%region_5.6 | all-reduce | flops 8192 | bytes 65536 | tf_op jit(solution)/shard_map/psum | solution.py:403
  246.3 0.9 reshape_squeeze.15
  247.2 0.9 reshape_squeeze.14
  248.0 1.6 dynamic-slice_maximum_fusion
  249.6 1.1 slice_reduce_fusion
  250.8 5.3 %all-to-all-start.7 = ((bf16[8,512,128]{2,1,0:T(8,128)(2,1)}), bf16[8,512,128]{2,1,0:T(8,128)(2,1)}, u32[]{:S(2)}, u32[]{:S(2)}) async-start(bf16[8,512,128]{2,1,0:T(8,128)(2,1)} %get-tuple-element.19), calls=%async_computation.7 | async-start | bytes 2097152 | tf_op jit(solution)/shard_map/all_to_all | solution.py:340
  256.3 1.1 slice_reduce_fusion.8
  257.4 0.4 copy-done.5
  257.9 2.2 fusion.5
  260.1 20.5 %all-to-all-done.7.heads_ref = bf16[8,512,128]{2,1,0:T(8,128)(2,1)} async-done(((bf16[8,512,128]{2,1,0:T(8,128)(2,1)}), bf16[8,512,128]{2,1,0:T(8,128)(2,1)}, u32[]{:S(2)}, u32[]{:S(2)}) %all-to-all-start.7) | async-done | bytes 1048608 | tf_op jit(solution)/shard_map/all_to_all | solution.py:340
  280.5 4.2 %all-to-all-start.6 = ((bf16[8,512,128]{2,1,0:T(8,128)(2,1)}), bf16[8,512,128]{2,1,0:T(8,128)(2,1)}, u32[]{:S(2)}, u32[]{:S(2)}) async-start(bf16[8,512,128]{2,1,0:T(8,128)(2,1)} %fusion.5), calls=%async_computation.6 | async-start | bytes 2097152 | tf_op jit(solution)/shard_map/all_to_all | solution.py:340
  285.0 2.0 fusion.2
  287.0 23.1 %all-to-all-done.6.heads_ref = bf16[8,512,128]{2,1,0:T(8,128)(2,1)} async-done(((bf16[8,512,128]{2,1,0:T(8,128)(2,1)}), bf16[8,512,128]{2,1,0:T(8,128)(2,1)}, u32[]{:S(2)}, u32[]{:S(2)}) %all-to-all-start.6) | async-done | bytes 1048608 | tf_op jit(solution)/shard_map/all_to_all | solution.py:340
  310.1 3.8 %all-to-all-start.5 = ((bf16[8,512,128]{2,1,0:T(8,128)(2,1)}), bf16[8,512,128]{2,1,0:T(8,128)(2,1)S(1)}, u32[]{:S(2)}, u32[]{:S(2)}) async-start(bf16[8,512,128]{2,1,0:T(8,128)(2,1)} %fusion.2), calls=%async_computation.5 | async-start | bytes 2097152 | tf_op jit(solution)/shard_map/all_to_all | solution.py:340
  313.9 3.2 shard_map.115
  317.1 3.2 shard_map.120
  320.3 3.2 shard_map.119
  323.4 16.2 %all-to-all-done.5.heads_ref = bf16[8,512,128]{2,1,0:T(8,128)(2,1)S(1)} async-done(((bf16[8,512,128]{2,1,0:T(8,128)(2,1)}), bf16[8,512,128]{2,1,0:T(8,128)(2,1)S(1)}, u32[]{:S(2)}, u32[]{:S(2)}) %all-to-all-start.5) | async-done | bytes 1048608 | tf_op jit(solution)/shard_map/all_to_all | solution.py:340
  339.6 1.0 copy-done.9
  340.6 3.2 shard_map.118
  (123 shorter events, 2.9 us)
Async XLA Ops:
  3.8 10.6 %copy-start.6 = (bf16[512,1024]{1,0:T(8,128)(2,1)S(1)}, bf16[512,1024]{1,0:T(8,128)(2,1)}, u32[]{:S(2)}) copy-start(bf16[512,1024]{1,0:T(8,128)(2,1)} %rows_ref.4) | copy-start | bytes 3145732
  3.8 33.2 %all-to-all-start.2 = ((bf16[8,512,128]{2,1,0:T(8,128)(2,1)}), bf16[8,512,128]{2,1,0:T(8,128)(2,1)S(1)}, u32[]{:S(2)}, u32[]{:S(2)}) async-start(bf16[8,512,128]{2,1,0:T(8,128)(2,1)} %shard_map.113), calls=%async_computation.2 | async-start | bytes 2097152 | tf_op jit(solution)/shard_map/all_to_all | solution.py:340
  14.4 27.1 %copy-start.7 = (bf16[512,1024]{1,0:T(8,128)(2,1)S(1)}, bf16[512,1024]{1,0:T(8,128)(2,1)}, u32[]{:S(2)}) copy-start(bf16[512,1024]{1,0:T(8,128)(2,1)} %rows_ref.5) | copy-start | bytes 3145732
  37.0 1.0 copy-start.10
  38.0 55.8 %all-to-all-start = ((bf16[8,512,128]{2,1,0:T(8,128)(2,1)}), bf16[8,512,128]{2,1,0:T(8,128)(2,1)S(1)}, u32[]{:S(2)}, u32[]{:S(2)}) async-start(bf16[8,512,128]{2,1,0:T(8,128)(2,1)} %shard_map.111), calls=%async_computation | async-start | bytes 2097152 | tf_op jit(solution)/shard_map/all_to_all | solution.py:340
  93.8 6.9 %copy-start = (bf16[8,512,128]{2,1,0:T(8,128)(2,1)}, bf16[8,512,128]{2,1,0:T(8,128)(2,1)S(1)}, u32[]{:S(2)}) copy-start(bf16[8,512,128]{2,1,0:T(8,128)(2,1)S(1)} %all-to-all-done) | copy-start | bytes 3145732
  93.8 24.4 %all-to-all-start.1 = ((bf16[8,512,128]{2,1,0:T(8,128)(2,1)}), bf16[8,512,128]{2,1,0:T(8,128)(2,1)S(1)}, u32[]{:S(2)}, u32[]{:S(2)}) async-start(bf16[8,512,128]{2,1,0:T(8,128)(2,1)} %shard_map.112), calls=%async_computation.1 | async-start | bytes 2097152 | tf_op jit(solution)/shard_map/all_to_all | solution.py:340
  118.2 7.3 %copy-start.2 = (bf16[8,512,128]{2,1,0:T(8,128)(2,1)}, bf16[8,512,128]{2,1,0:T(8,128)(2,1)S(1)}, u32[]{:S(2)}) copy-start(bf16[8,512,128]{2,1,0:T(8,128)(2,1)S(1)} %all-to-all-done.1) | copy-start | bytes 3145732
  118.2 39.3 %all-to-all-start.4 = ((bf16[8,512,128]{2,1,0:T(8,128)(2,1)}), bf16[8,512,128]{2,1,0:T(8,128)(2,1)S(1)}, u32[]{:S(2)}, u32[]{:S(2)}) async-start(bf16[8,512,128]{2,1,0:T(8,128)(2,1)} %shard_map.116), calls=%async_computation.4 | async-start | bytes 2097152 | tf_op jit(solution)/shard_map/all_to_all | solution.py:340
  122.1 6.9 %copy-start.13 = (bf16[1024]{0:T(1024)(128)(2,1)S(1)}, bf16[1024]{0:T(1024)(128)(2,1)}, u32[]{:S(2)}) copy-start(bf16[1024]{0:T(1024)(128)(2,1)} %param.11) | copy-start | bytes 6148
  122.1 7.6 %copy-start.14 = (bf16[1024]{0:T(1024)(128)(2,1)S(1)}, bf16[1024]{0:T(1024)(128)(2,1)}, u32[]{:S(2)}) copy-start(bf16[1024]{0:T(1024)(128)(2,1)} %param.12) | copy-start | bytes 6148
  157.5 5.7 %copy-start.11 = (bf16[8,512,128]{2,1,0:T(8,128)(2,1)}, bf16[8,512,128]{2,1,0:T(8,128)(2,1)S(1)}, u32[]{:S(2)}) copy-start(bf16[8,512,128]{2,1,0:T(8,128)(2,1)S(1)} %all-to-all-done.4) | copy-start | bytes 3145732
  157.5 93.3 %all-to-all-start.3 = ((bf16[8,512,128]{2,1,0:T(8,128)(2,1)}), bf16[8,512,128]{2,1,0:T(8,128)(2,1)S(1)}, u32[]{:S(2)}, u32[]{:S(2)}) async-start(bf16[8,512,128]{2,1,0:T(8,128)(2,1)} %get-tuple-element.12), calls=%async_computation.3 | async-start | bytes 2097152 | tf_op jit(solution)/shard_map/all_to_all | solution.py:340
  163.2 34.1 %copy-start.1 = (bf16[8,512,128]{2,1,0:T(8,128)(2,1)S(1)}, bf16[8,512,128]{2,1,0:T(8,128)(2,1)}, u32[]{:S(2)}) copy-start(bf16[8,512,128]{2,1,0:T(8,128)(2,1)} %copy-done) | copy-start | bytes 3145732
  197.3 2.4 copy-start.3
  202.2 0.6 copy-start.12
  250.8 6.6 %copy-start.8 = (bf16[8,512,128]{2,1,0:T(8,128)(2,1)}, bf16[8,512,128]{2,1,0:T(8,128)(2,1)S(1)}, u32[]{:S(2)}) copy-start(bf16[8,512,128]{2,1,0:T(8,128)(2,1)S(1)} %all-to-all-done.3.heads_ref) | copy-start | bytes 3145732
  250.8 29.7 %all-to-all-start.7 = ((bf16[8,512,128]{2,1,0:T(8,128)(2,1)}), bf16[8,512,128]{2,1,0:T(8,128)(2,1)}, u32[]{:S(2)}, u32[]{:S(2)}) async-start(bf16[8,512,128]{2,1,0:T(8,128)(2,1)} %get-tuple-element.19), calls=%async_computation.7 | async-start | bytes 2097152 | tf_op jit(solution)/shard_map/all_to_all | solution.py:340
  256.3 1.6 copy-start.5
  260.1 24.9 %copy-start.4 = (f32[8,512,128]{2,1,0:T(8,128)S(1)}, f32[8,512,128]{2,1,0:T(8,128)}, u32[]{:S(2)}) copy-start(f32[8,512,128]{2,1,0:T(8,128)} %get-tuple-element.17) | copy-start | bytes 6291460
  280.5 29.6 %all-to-all-start.6 = ((bf16[8,512,128]{2,1,0:T(8,128)(2,1)}), bf16[8,512,128]{2,1,0:T(8,128)(2,1)}, u32[]{:S(2)}, u32[]{:S(2)}) async-start(bf16[8,512,128]{2,1,0:T(8,128)(2,1)} %fusion.5), calls=%async_computation.6 | async-start | bytes 2097152 | tf_op jit(solution)/shard_map/all_to_all | solution.py:340
  310.1 29.5 %all-to-all-start.5 = ((bf16[8,512,128]{2,1,0:T(8,128)(2,1)}), bf16[8,512,128]{2,1,0:T(8,128)(2,1)S(1)}, u32[]{:S(2)}, u32[]{:S(2)}) async-start(bf16[8,512,128]{2,1,0:T(8,128)(2,1)} %fusion.2), calls=%async_computation.5 | async-start | bytes 2097152 | tf_op jit(solution)/shard_map/all_to_all | solution.py:340
  339.6 1.0 copy-start.9

commit v2 on v1

--- a/solution.py
+++ b/solution.py
@@ -57,7 +57,7 @@
     return 0 if heads % CLASSES == 0 else lax.axis_index("head") * heads % CLASSES
 
 
-def split_kernel(matrix_ref, rows_ref, heads_ref, sorted_ref):
+def split_rows(matrix_ref, rows_ref, sorted_ref, heads_ref):
     heads = heads_ref.shape[0]
     first_head = first_class(heads)
     sorted_ref[...] = dot_nn(matrix_ref[...], rows_ref[...]).astype(jnp.bfloat16)
@@ -68,8 +68,8 @@
             ]
 
 
-def join_kernel(matrix_ref, heads_ref, rows_ref, sorted_ref):
-    heads = heads_ref.shape[0]
+def join_rows(matrix_ref, heads_ref, sorted_ref, rows_ref):
+    heads = rows_ref.shape[1] // DH
     first_head = first_class(heads)
     for head in range(heads):
         for place, residue in enumerate(ORDER):
@@ -79,7 +79,182 @@
     rows_ref[...] = dot_tn(matrix_ref[...], sorted_ref[...]).astype(jnp.bfloat16)
 
 
-def vmem_call(kernel, outs, scratch=(), operand_count=0, smem_first=False, flops=0):
+def peers_of(axis):
+    count, place = lax.axis_size(axis), lax.axis_index(axis)
+    return [(step, (place + step) % count) for step in range(1, count)]
+
+
+def meet_peers():
+    barrier = pltpu.get_barrier_semaphore()
+    total = 0
+    for axis in ("ctx", "head"):
+        for _, peer in peers_of(axis):
+            pl.semaphore_signal(barrier, inc=1, device_id={axis: peer}, device_id_type=pl.DeviceIdType.MESH)
+            total += 1
+    pl.semaphore_wait(barrier, total)
+
+
+def send_all(axis, source_of, target, sems):
+    copies = []
+    for step, peer in peers_of(axis):
+        copy = pltpu.make_async_remote_copy(
+            src_ref=source_of(peer),
+            dst_ref=target,
+            send_sem=sems.at[0, step],
+            recv_sem=sems.at[1, step],
+            device_id={axis: peer},
+            device_id_type=pl.DeviceIdType.MESH,
+        )
+        copy.start()
+        copies.append(copy)
+    return copies
+
+
+def receive_all(copies):
+    for copy in copies:
+        copy.wait_recv()
+
+
+def finish_sends(copies):
+    for copy in copies:
+        copy.wait_send()
+
+
+def head_residue(heads_local):
+    return (lax.axis_index("head") * heads_local + lax.axis_index("ctx") % heads_local) % CLASSES
+
+
+def row_sums(rows):
+    return jnp.sum(rows.T, axis=0, keepdims=True)
+
+
+def columns(row):
+    return jnp.broadcast_to(row, (DH, PER)).T
+
+
+def inbound_kernel(
+    matrix_ref, query_ref, key_ref, value_ref, grad_ref, query_gain_ref, key_gain_ref,
+    qn_ref, kn_ref, qh_ref, kh_ref, vh_ref, grad_heads_ref, inverse_ref,
+    sorted_ref, send_ref, sums_ref, query_sems, key_sems, value_sems, sums_sems, inverse_sems,
+):
+    segs, heads_local = vh_ref.shape[0], grad_heads_ref.shape[0]
+    me, my_group = lax.axis_index("ctx"), lax.axis_index("head")
+    residue = head_residue(heads_local)
+    meet_peers()
+    sends = []
+    for index, (rows_ref, arrived_ref, sems) in enumerate(
+        ((query_ref, qh_ref, query_sems), (key_ref, kh_ref, key_sems), (value_ref, vh_ref, value_sems))
+    ):
+        split_rows(matrix_ref, rows_ref, sorted_ref, send_ref.at[index])
+        sends.append(
+            send_all("ctx", lambda peer: send_ref.at[index, peer % heads_local], arrived_ref.at[me], sems)
+        )
+        arrived_ref[me] = send_ref[index, me % heads_local]
+        if index < 2:
+            squares = jnp.zeros((SEG, DH), jnp.float32)
+            for head in range(heads_local):
+                block = sorted_ref[:, head * DH : (head + 1) * DH].astype(jnp.float32)
+                squares = squares + block * block
+            for place in range(CLASSES):
+                sums_ref[my_group, index, place : place + 1, :] = row_sums(squares[place * PER : (place + 1) * PER])
+        if index == 1:
+            sums_sends = send_all("head", lambda peer: sums_ref.at[my_group], sums_ref.at[my_group], sums_sems)
+    receive_all(sums_sends)
+    total = sums_ref[0]
+    for group in range(1, sums_ref.shape[0]):
+        total = total + sums_ref[group]
+    inverse_ref[me] = lax.rsqrt(total / D + EPSILON)
+    inverse_sends = send_all("ctx", lambda peer: inverse_ref.at[me], inverse_ref.at[me], inverse_sems)
+    split_rows(matrix_ref, grad_ref, sorted_ref, grad_heads_ref)
+    receive_all(inverse_sends)
+    for index, (arrived_ref, gain_ref, normed_ref) in enumerate(
+        ((qh_ref, query_gain_ref, qn_ref), (kh_ref, key_gain_ref, kn_ref))
+    ):
+        receive_all(sends[index])
+
+        def normalise(seg, carry):
+            for place in range(CLASSES):
+                rows = slice(place * PER, (place + 1) * PER)
+                inverse = inverse_ref[seg, index, pl.ds((residue + ORDER[place]) % CLASSES, 1), :]
+                normed = arrived_ref[seg, rows, :].astype(jnp.float32) * columns(inverse) * gain_ref[...]
+                normed_ref[seg, rows, :] = normed.astype(jnp.bfloat16)
+            return carry
+
+        lax.fori_loop(0, segs, normalise, 0)
+    receive_all(sends[2])
+    for copies in sends + [sums_sends, inverse_sends]:
+        finish_sends(copies)
+
+
+def outbound_kernel(
+    matrix_ref, attended_ref, dv_ref, dq_ref, dk_ref, qh_ref, kh_ref, inverse_ref, query_gain_ref, key_gain_ref,
+    out_ref, query_grads_ref, key_grads_ref, value_grads_ref,
+    sorted_ref, send_ref, arrived_ref, inner_ref, inner_in_ref, group_ref, total_ref,
+    query_sems, key_sems, value_sems, inner_sems, group_sems, total_sems,
+):
+    segs, heads_local = dv_ref.shape[0], out_ref.shape[1] // DH
+    me, my_group = lax.axis_index("ctx"), lax.axis_index("head")
+    residue = head_residue(heads_local)
+    pairs = ((qh_ref, dq_ref, query_gain_ref), (kh_ref, dk_ref, key_gain_ref))
+    meet_peers()
+    sends = [send_all("ctx", lambda peer: dv_ref.at[peer], arrived_ref.at[2, me], value_sems)]
+    arrived_ref[2, me] = dv_ref[me]
+
+    def inner_products(seg, carry):
+        for index, (raw_ref, grad_ref, gain_ref) in enumerate(pairs):
+            for place in range(CLASSES):
+                rows = slice(place * PER, (place + 1) * PER)
+                product = raw_ref[seg, rows, :].astype(jnp.float32) * (gain_ref[...] * grad_ref[seg, rows, :])
+                inner_ref[seg, index, pl.ds((residue + ORDER[place]) % CLASSES, 1), :] = row_sums(product)
+        return carry
+
+    lax.fori_loop(0, segs, inner_products, 0)
+    inner_sends = send_all("ctx", lambda peer: inner_ref.at[peer], inner_in_ref.at[me], inner_sems)
+    inner_in_ref[me] = inner_ref[me]
+    receive_all(inner_sends)
+    subtotal = inner_in_ref[0]
+    for head in range(1, heads_local):
+        subtotal = subtotal + inner_in_ref[head]
+    group_ref[my_group] = subtotal
+    group_sends = send_all("head", lambda peer: group_ref.at[my_group], group_ref.at[my_group], group_sems)
+    receive_all(group_sends)
+    total = group_ref[0]
+    for group in range(1, group_ref.shape[0]):
+        total = total + group_ref[group]
+    total_ref[me] = total
+    total_sends = send_all("ctx", lambda peer: total_ref.at[me], total_ref.at[me], total_sems)
+    join_rows(matrix_ref, attended_ref, sorted_ref, out_ref)
+    receive_all(total_sends)
+    for index, (raw_ref, grad_ref, gain_ref) in enumerate(pairs):
+
+        def final_grads(seg, carry):
+            inverse = inverse_ref[seg, index]
+            weight = inverse * inverse * inverse * total_ref[seg, index] / D
+            inner_ref[seg, index] = weight
+            for place in range(CLASSES):
+                rows = slice(place * PER, (place + 1) * PER)
+                pick = pl.ds((residue + ORDER[place]) % CLASSES, 1)
+                adjoint = gain_ref[...] * grad_ref[seg, rows, :]
+                raw = raw_ref[seg, rows, :].astype(jnp.float32)
+                grads = columns(inverse_ref[seg, index, pick, :]) * adjoint
+                grads = grads - raw * columns(inner_ref[seg, index, pick, :])
+                send_ref[index, seg, rows, :] = grads.astype(jnp.bfloat16)
+            return carry
+
+        if index == 0:
+            finish_sends(inner_sends)
+        lax.fori_loop(0, segs, final_grads, 0)
+        sems = (query_sems, key_sems)[index]
+        sends.append(send_all("ctx", lambda peer: send_ref.at[index, peer], arrived_ref.at[index, me], sems))
+        arrived_ref[index, me] = send_ref[index, me]
+    for copies, slot, rows_ref in zip(sends, (2, 0, 1), (value_grads_ref, query_grads_ref, key_grads_ref)):
+        receive_all(copies)
+        join_rows(matrix_ref, arrived_ref.at[slot], sorted_ref, rows_ref)
+    for copies in sends + [group_sends, total_sends]:
+        finish_sends(copies)
+
+
+def vmem_call(kernel, outs, scratch=(), operand_count=0, smem_first=False, flops=0, collective_id=None):
     specs = [pl.BlockSpec(memory_space=pltpu.VMEM)] * operand_count
     if smem_first:
         specs = [pl.BlockSpec(memory_space=pltpu.SMEM)] + specs[1:]
@@ -90,22 +265,12 @@
         out_specs=jax.tree.map(lambda _: pl.BlockSpec(memory_space=pltpu.VMEM), outs),
         scratch_shapes=list(scratch),
         cost_estimate=pl.CostEstimate(flops=flops, bytes_accessed=2**23, transcendentals=flops // 512),
-        compiler_params=pltpu.CompilerParams(vmem_limit_bytes=VMEM_BYTES),
+        compiler_params=pltpu.CompilerParams(
+            vmem_limit_bytes=VMEM_BYTES,
+            collective_id=collective_id,
+            has_side_effects=collective_id is not None,
+        ),
     )
-
-
-def split_heads(matrix, rows):
-    width = rows.shape[1]
-    out = jax.ShapeDtypeStruct((width // DH, SEG, DH), jnp.bfloat16)
-    scratch = [pltpu.VMEM((SEG, width), jnp.bfloat16)]
-    return vmem_call(split_kernel, out, scratch, operand_count=2, flops=2 * SEG * SEG * width)(matrix, rows)
-
-
-def join_heads(matrix, heads):
-    width = heads.shape[0] * DH
-    out = jax.ShapeDtypeStruct((SEG, width), jnp.bfloat16)
-    scratch = [pltpu.VMEM((SEG, width), jnp.bfloat16)]
-    return vmem_call(join_kernel, out, scratch, operand_count=2, flops=2 * SEG * SEG * width)(matrix, heads)
 
 
 def take_block(ref, block):
@@ -147,21 +312,9 @@
 
 
 def forward_kernel(
-    slots, blocks_ref, query_ref, key_ref, value_ref, query_r_ref, key_r_ref, query_gain_ref, key_gain_ref,
-    out_ref, merged_ref, lse_ref, qn_ref, kn_ref, max_ref, total_ref,
+    slots, blocks_ref, qn_ref, kn_ref, value_ref, out_ref, merged_ref, lse_ref, max_ref, total_ref,
 ):
-    segs = query_ref.shape[0]
-
-    def normalise(seg, carry):
-        for raw, inverse, gain, normed in (
-            (query_ref, query_r_ref, query_gain_ref, qn_ref),
-            (key_ref, key_r_ref, key_gain_ref, kn_ref),
-        ):
-            rows = raw[seg].reshape(SEG, DH).astype(jnp.float32) * inverse[seg] * gain[...]
-            normed[seg] = rows.astype(jnp.bfloat16).reshape(CLASSES, PER, DH)
-        return carry
-
-    lax.fori_loop(0, segs, normalise, 0)
+    segs = qn_ref.shape[0]
 
     def own_and_memory(seg, carry):
         query_rows = take_rows(qn_ref, [seg], CLASSES)
@@ -323,64 +476,45 @@
     lax.fori_loop(0, segs, finish, 0)
 
 
-def to_head_order(vector, head):
-    parts = vector.reshape(-1, PER, CLASSES)
-    rolled = lax.dynamic_slice_in_dim(jnp.concatenate([parts, parts], axis=2), head, CLASSES, axis=2)
-    return jnp.stack([rolled[:, :, residue] for residue in ORDER], axis=1).reshape(vector.shape)
-
-
-def from_head_order(vector, head):
-    parts = vector.reshape(-1, CLASSES, PER)
-    natural = jnp.stack([parts[:, ORDER.index(residue)] for residue in range(CLASSES)], axis=2)
-    doubled = jnp.concatenate([natural, natural], axis=2)
-    return lax.dynamic_slice_in_dim(doubled, (CLASSES - head) % CLASSES, CLASSES, axis=2).reshape(vector.shape)
-
-
 def exchange(heads):
     return lax.all_to_all(heads, "ctx", split_axis=0, concat_axis=0, tiled=True)
-
-
-def send_heads(heads):
-    return exchange(jnp.concatenate([heads] * (lax.axis_size("ctx") // heads.shape[0]), axis=0))
 
 
 def head_shards(queries, key_states, values, query_gain, key_gain, memory_blocks, cotangent):
     segs, slots = memory_blocks.shape
     heads_local = queries.shape[1] // DH
     local_head = lax.axis_index("ctx") % heads_local
-    head = (lax.axis_index("head") * heads_local + local_head) % CLASSES
+    groups = lax.axis_size("head")
     matrix = class_matrix()
-    query_heads = send_heads(split_heads(matrix, queries))
-    key_heads = send_heads(split_heads(matrix, key_states))
-    value_heads = send_heads(split_heads(matrix, values))
-    grad_heads = send_heads(split_heads(matrix, cotangent))
-    squares = jnp.stack(
-        [jnp.sum(jnp.square(rows.astype(jnp.float32)), axis=1) for rows in (queries, key_states)]
-    )
-    squares = lax.psum(squares, "head")
-    squares = lax.all_gather(squares, "ctx", axis=1)
-    inverse = lax.rsqrt(squares / D + EPSILON)
-    inverse = jnp.stack([to_head_order(inverse[0], head), to_head_order(inverse[1], head)])
     gains = [
         lax.dynamic_slice_in_dim(gain, local_head * DH, DH).astype(jnp.float32)[None, :]
         for gain in (query_gain, key_gain)
     ]
     classed = (segs, CLASSES, PER, DH)
     flat = (segs, SEG, DH)
+    width = heads_local * DH
+    sums = (2, CLASSES, PER)
     shape = jax.ShapeDtypeStruct
+    ctx_sems, head_sems = pltpu.SemaphoreType.DMA((2, segs)), pltpu.SemaphoreType.DMA((2, groups))
     pairs = segs * SEG * SEG * 4
-    attended, merged, lse, query_normed, key_normed = vmem_call(
+    query_normed, key_normed, query_heads, key_heads, value_heads, grad_heads, inverse = vmem_call(
+        inbound_kernel,
+        (shape(flat, jnp.bfloat16),) * 5
+        + (shape((heads_local, SEG, DH), jnp.bfloat16), shape((segs,) + sums, jnp.float32)),
+        [
+            pltpu.VMEM((SEG, width), jnp.bfloat16), pltpu.VMEM((3, heads_local, SEG, DH), jnp.bfloat16),
+            pltpu.VMEM((groups,) + sums, jnp.float32), ctx_sems, ctx_sems, ctx_sems, head_sems, ctx_sems,
+        ],
+        operand_count=7, flops=8 * SEG * SEG * width, collective_id=0,
+    )(matrix, queries, key_states, values, cotangent, *gains)
+    grad_heads = exchange(jnp.concatenate([grad_heads] * (segs // heads_local), axis=0))
+    query_normed, key_normed = query_normed.reshape(classed), key_normed.reshape(classed)
+    attended, merged, lse = vmem_call(
         functools.partial(forward_kernel, slots),
-        (
-            shape(flat, jnp.bfloat16), shape((segs, DH, SEG), jnp.float32), shape((segs, 1, SEG), jnp.float32),
-            shape(classed, jnp.bfloat16), shape(classed, jnp.bfloat16),
-        ),
+        (shape(flat, jnp.bfloat16), shape((segs, DH, SEG), jnp.float32), shape((segs, 1, SEG), jnp.float32)),
         [pltpu.VMEM((segs, 1, SEG), jnp.float32)] * 2,
-        operand_count=8, smem_first=True, flops=pairs * DH * 4,
-    )(
-        memory_blocks, query_heads.reshape(classed), key_heads.reshape(classed), value_heads.reshape(classed),
-        inverse[0][:, :, None], inverse[1][:, :, None], *gains,
-    )
+        operand_count=4, smem_first=True, flops=pairs * DH * 4,
+    )(memory_blocks, query_normed, key_normed, value_heads.reshape(classed))
     attended = exchange(attended)
     dq, dk, dv = vmem_call(
         functools.partial(backward_kernel, slots),
@@ -394,19 +528,18 @@
         memory_blocks, query_normed, key_normed, value_heads.reshape(classed), grad_heads.reshape(classed),
         merged, lse,
     )
-    value_grads = exchange(dv)
-    raw = [query_heads.astype(jnp.float32), key_heads.astype(jnp.float32)]
-    adjoint = [gains[0] * dq, gains[1] * dk.reshape(flat)]
-    inner = jnp.stack([from_head_order(jnp.sum(raw[i] * adjoint[i], axis=2), head) for i in range(2)])
-    if segs > heads_local:
-        inner = jnp.where(lax.axis_index("ctx") < heads_local, inner, 0.0)
-    inner = lax.psum(inner, ("ctx", "head"))
-    grads = []
-    for i in range(2):
-        scale = inverse[i][:, :, None]
-        weight = inverse[i] ** 3 * to_head_order(inner[i], head) / D
-        grads.append(exchange((scale * adjoint[i] - raw[i] * weight[:, :, None]).astype(jnp.bfloat16)))
-    return tuple(join_heads(matrix, heads[:heads_local]) for heads in (attended, grads[0], grads[1], value_grads))
+    return vmem_call(
+        outbound_kernel,
+        (shape((SEG, width), jnp.bfloat16),) * 4,
+        [
+            pltpu.VMEM((SEG, width), jnp.bfloat16), pltpu.VMEM((2,) + flat, jnp.bfloat16),
+            pltpu.VMEM((3,) + flat, jnp.bfloat16), pltpu.VMEM((segs,) + sums, jnp.float32),
+            pltpu.VMEM((segs,) + sums, jnp.float32), pltpu.VMEM((groups,) + sums, jnp.float32),
+            pltpu.VMEM((segs,) + sums, jnp.float32),
+            ctx_sems, ctx_sems, ctx_sems, ctx_sems, head_sems, ctx_sems,
+        ],
+        operand_count=10, flops=8 * SEG * SEG * width, collective_id=1,
+    )(matrix, attended, dv, dq, dk.reshape(flat), query_heads, key_heads, inverse, *gains)
 
 
 def solution(mesh):

time: 345 us -> 252 us (0.73)
  Pallas kernels: 86.6 us -> 229 us
  waiting for transfers between devices: 99.5 us -> 1.77 us
  blocking collectives: 86.5 us -> 0 us
  starting transfers between devices: 37.5 us -> 8.46 us
  local copies, waits for them, and re-layouts: 19.5 us -> 6.3 us
  other arithmetic: 12.8 us -> 1.32 us
    pallas_call x8 -> x2, Pallas kernels: 25.5 us -> 172 us  [the longest x1 85.9 us: head_shards(): vmem_call(inbound_kernel, (shape(flat, jnp.bfloat16),) * 5 + (shape((head...]
    all_to_all x8 -> x2, waiting for transfers between devices: 99.5 us -> 1.77 us  [exchange(): return lax.all_to_all(heads, 'ctx', split_axis=0, concat_axis=0, tiled=True)]
    psum x2 -> x0, blocking collectives: 47.7 us -> none  [the longest x1 40.9 us: head_shards(): inner = lax.psum(inner, ('ctx', 'head'))]
    all_gather x1 -> x0, blocking collectives: 38.8 us -> none  [head_shards(): squares = lax.all_gather(squares, 'ctx', axis=1)]
    all_to_all x8 -> x2, starting transfers between devices: 37.5 us -> 8.46 us  [exchange(): return lax.all_to_all(heads, 'ctx', split_axis=0, concat_axis=0, tiled=True)]
    another operation x16 -> x0, local copies, waits for them, and re-layouts: 9.22 us -> none  [the longest x1 3.42 us: head_shards(): inverse[1][:, :, None]]
    reduce_sum x4 -> x0, other arithmetic: 5.07 us -> none  [the longest x2 4.51 us: head_shards(): jnp.sum(raw[i] * adjoint[i], axis=2)]
    slice x8 -> x0, local copies, waits for them, and re-layouts: 4.55 us -> none  [the longest x4 4.41 us: to_head_order(): rolled[:, :, residue]]
  transfers between devices with their start and end apart: 8 -> 2, of which waited for: 5 -> 1; matrix products, arithmetic and copies ran while one was open for 9% -> 0% of each run, Pallas kernels for 23% -> 23%
where the time goes in v2:
time: 252 us; the launch traced here: 247 us
  Pallas kernels  229 us (91%)
  starting transfers between devices  8.46 us (3%)
  local copies, waits for them, and re-layouts  6.3 us (2%)
    pallas_call x1, Pallas kernels, head_shards(): vmem_call(inbound_kernel, (shape(flat, jnp.bfloat16),) * 5 + (shape((head...  85.9 us
    pallas_call x1, Pallas kernels, head_shards(): vmem_call(outbound_kernel, (shape((SEG, width), jnp.bfloat16),) * 4, [plt...  85.8 us
    pallas_call x1, Pallas kernels, head_shards(): vmem_call(functools.partial(backward_kernel, slots), (shape(flat, jnp.flo...  33.8 us
    pallas_call x1, Pallas kernels, head_shards(): vmem_call(functools.partial(forward_kernel, slots), (shape(flat, jnp.bflo...  23.4 us
    all_to_all x2, starting transfers between devices, exchange(): return lax.all_to_all(heads, 'ctx', split_axis=0, concat_axis=0, tiled=True)  8.46 us
    unnamed x14, local copies, waits for them, and re-layouts  6.3 us
  transfers between devices with their start and end apart: 2, of which 1 were waited for; matrix products, arithmetic and copies ran while one was open for 0% of the time, Pallas kernels for 23%

profile of v2, /device:TPU:0, one launch (start us, length us, event | category | flops | bytes accessed | tf_op | source)
XLA Modules:
  0.0 247.4 jit_solution(12064724564304497027)
XLA Ops:
  0.6 1.3 bitcast_convert_fusion
  2.0 85.9 %shard_map.111 = (bf16[8,512,128]{2,1,0:T(8,128)(2,1)}, bf16[8,512,128]{2,1,0:T(8,128)(2,1)}, bf16[8,512,128]{2,1,0:T(8,128)(2,1)}, bf16[8,512,128]{2,1,0:T(8,12...) custom-call(bf16[512,512]{1,0:T(8,128)(2,1)} %constant.26.clone.matrix_ref, ...), custom_call_target="tpu_custom_call" | custom-call | flops 2147483648 | bytes 8388608 | tf_op jit(solution)/shard_map/pallas_call | solution.py:500
  87.8 4.2 %all-to-all-start.1 = ((bf16[8,512,128]{2,1,0:T(8,128)(2,1)}), bf16[8,512,128]{2,1,0:T(8,128)(2,1)S(1)}, u32[]{:S(2)}, u32[]{:S(2)}) async-start(bf16[8,512,128]{2,1,0:T(8,128)(2,1)} %get-tuple-element.21), calls=%async_computation.1 | async-start | bytes 2097152 | tf_op jit(solution)/shard_map/all_to_all | solution.py:480
  92.0 23.4 %shard_map.112 = (bf16[8,512,128]{2,1,0:T(8,128)(2,1)}, f32[8,128,512]{2,1,0:T(8,128)}, f32[8,1,512]{2,1,0:T(1,128)}) custom-call(s32[8,8]{1,0:T(8,128)} %blocks_ref.3, bf16[8,8,64,128]{3,2,1,0:T(8,128)(2,1)} %bitcast.13, bf16[8,8,64,128]{3,2,1,0:T(8,128)(2,1)} %bitcast.15, bf16[8,8,64,128]{3,2,1,0:T(8,128)(2,1)} %bitcast.17), custom_call_target="tpu_custom_call" | custom-call | flops 4294967296 | bytes 8388608 | tf_op jit(solution)/shard_map/pallas_call | solution.py:512
  115.4 1.8 all-to-all-done.1
  117.2 0.0 copy-start.1
  117.2 4.3 %all-to-all-start = ((bf16[8,512,128]{2,1,0:T(8,128)(2,1)}), bf16[8,512,128]{2,1,0:T(8,128)(2,1)S(1)}, u32[]{:S(2)}, u32[]{:S(2)}) async-start(bf16[8,512,128]{2,1,0:T(8,128)(2,1)} %get-tuple-element.20), calls=%async_computation | async-start | bytes 2097152 | tf_op jit(solution)/shard_map/all_to_all | solution.py:480
  121.4 0.0 copy-done.1
  121.4 33.8 %shard_map.113 = (f32[8,512,128]{2,1,0:T(8,128)}, f32[8,8,64,128]{3,2,1,0:T(8,128)}, bf16[8,512,128]{2,1,0:T(8,128)(2,1)}) custom-call(s32[8,8]{1,0:T(8,128)} %blocks_ref.3, bf16[8,8,64,128]{3,2,1,0:T(8,128)(2,1)} %bitcast.14, bf16[8,8,64,128]{3,2,1,0:T(8,128)(2,1)} %bitcast.16, bf16[8,8,64,128]{3,2,1,0:T(8,128)(2,1)} %bitcast.18, ...), custom_call_target="tpu_custom_call" | custom-call | flops 10737418240 | bytes 8388608 | tf_op jit(solution)/shard_map/pallas_call | solution.py:519
  155.3 0.0 all-to-all-done.attended_ref
  155.3 0.0 copy-start
  155.3 1.0 copy-done
  156.2 85.8 %shard_map.114 = (bf16[512,1024]{1,0:T(8,128)(2,1)}, bf16[512,1024]{1,0:T(8,128)(2,1)}, bf16[512,1024]{1,0:T(8,128)(2,1)}, bf16[512,1024]{1,0:T(8,128)(2,1)}) custom-call(bf16[512,512]{1,0:T(8,128)(2,1)} %constant.26.clone.matrix_ref, bf16[8,512,128]{2,1,0:T(8,128)(2,1)} %copy-done, bf16[8,512,128]{2,1,0:T(8,128)(2,1)} %get-tuple-element.24.dv_ref, ...), custom_call_target="tpu_custom_call" | custom-call | flops 2147483648 | bytes 8388608 | tf_op jit(solution)/shard_map/pallas_call | solution.py:531
  242.1 0.0 copy-start.4
  242.1 0.0 copy-start.3
  242.1 2.4 copy.16
  244.5 0.0 copy-done.4
  244.5 0.0 copy-start.2
  244.5 1.0 copy.17
  245.5 0.0 copy-done.3
  245.5 1.0 copy.18
  246.5 0.0 copy-done.2
  246.5 1.0 copy.19
Async XLA Ops:
  87.8 29.3 %all-to-all-start.1 = ((bf16[8,512,128]{2,1,0:T(8,128)(2,1)}), bf16[8,512,128]{2,1,0:T(8,128)(2,1)S(1)}, u32[]{:S(2)}, u32[]{:S(2)}) async-start(bf16[8,512,128]{2,1,0:T(8,128)(2,1)} %get-tuple-element.21), calls=%async_computation.1 | async-start | bytes 2097152 | tf_op jit(solution)/shard_map/all_to_all | solution.py:480
  117.2 4.3 %copy-start.1 = (bf16[8,512,128]{2,1,0:T(8,128)(2,1)}, bf16[8,512,128]{2,1,0:T(8,128)(2,1)S(1)}, u32[]{:S(2)}) copy-start(bf16[8,512,128]{2,1,0:T(8,128)(2,1)S(1)} %all-to-all-done.1) | copy-start | bytes 3145732
  117.2 38.1 %all-to-all-start = ((bf16[8,512,128]{2,1,0:T(8,128)(2,1)}), bf16[8,512,128]{2,1,0:T(8,128)(2,1)S(1)}, u32[]{:S(2)}, u32[]{:S(2)}) async-start(bf16[8,512,128]{2,1,0:T(8,128)(2,1)} %get-tuple-element.20), calls=%async_computation | async-start | bytes 2097152 | tf_op jit(solution)/shard_map/all_to_all | solution.py:480
  155.3 1.0 copy-start
  242.1 2.4 copy-start.4
  242.1 3.4 %copy-start.3 = (bf16[512,1024]{1,0:T(8,128)(2,1)S(1)}, bf16[512,1024]{1,0:T(8,128)(2,1)}, u32[]{:S(2)}) copy-start(bf16[512,1024]{1,0:T(8,128)(2,1)} %get-tuple-element.38) | copy-start | bytes 3145732
  244.5 1.9 copy-start.2

commit v3 on v2

--- a/solution.py
+++ b/solution.py
@@ -63,7 +63,7 @@
     sorted_ref[...] = dot_nn(matrix_ref[...], rows_ref[...]).astype(jnp.bfloat16)
     for head in range(heads):
         for place, residue in enumerate(ORDER):
-            heads_ref[head, place * PER : (place + 1) * PER, :] = sorted_ref[
+            heads_ref[head, place] = sorted_ref[
                 class_rows(first_head, head, residue), head * DH : (head + 1) * DH
             ]
 
@@ -79,9 +79,19 @@
     rows_ref[...] = dot_tn(matrix_ref[...], sorted_ref[...]).astype(jnp.bfloat16)
 
 
+def flip(place, mask, count):
+    flipped, bit = 0, 1
+    while bit < count:
+        flipped = flipped + bit * ((place // bit + mask // bit) % 2)
+        bit = 2 * bit
+    return flipped
+
+
 def peers_of(axis):
     count, place = lax.axis_size(axis), lax.axis_index(axis)
-    return [(step, (place + step) % count) for step in range(1, count)]
+    far, near = list(range(count - 1, count // 2 - 1, -1)), list(range(count // 2 - 1, 0, -1))
+    masks = [mask for pair in zip(far, near + [0]) for mask in pair if mask]
+    return [(mask, flip(place, mask, count)) for mask in masks]
 
 
 def meet_peers():
@@ -132,18 +142,30 @@
     return jnp.broadcast_to(row, (DH, PER)).T
 
 
+def store_block_rows(blocks_ref, seg, place, rows):
+    piece = BLOCK // CLASSES
+    for local in range(SEG // BLOCK):
+        blocks_ref[seg * (SEG // BLOCK) + local, place * piece : (place + 1) * piece, :] = rows[
+            local * piece : (local + 1) * piece
+        ]
+
+
 def inbound_kernel(
-    matrix_ref, query_ref, key_ref, value_ref, grad_ref, query_gain_ref, key_gain_ref,
-    qn_ref, kn_ref, qh_ref, kh_ref, vh_ref, grad_heads_ref, inverse_ref,
-    sorted_ref, send_ref, sums_ref, query_sems, key_sems, value_sems, sums_sems, inverse_sems,
+    slots, blocks_ref, matrix_ref, query_ref, key_ref, value_ref, grad_ref, query_gain_ref, key_gain_ref,
+    qn_ref, kn_ref, qh_ref, kh_ref, vh_ref, gh_ref, inverse_ref, out_ref, merged_ref, lse_ref,
+    sorted_ref, send_ref, sums_ref, kb_ref, vb_ref, max_ref, total_ref,
+    query_sems, key_sems, value_sems, grad_sems, sums_sems, inverse_sems,
 ):
-    segs, heads_local = vh_ref.shape[0], grad_heads_ref.shape[0]
+    segs, heads_local = vh_ref.shape[0], send_ref.shape[1]
     me, my_group = lax.axis_index("ctx"), lax.axis_index("head")
     residue = head_residue(heads_local)
     meet_peers()
     sends = []
     for index, (rows_ref, arrived_ref, sems) in enumerate(
-        ((query_ref, qh_ref, query_sems), (key_ref, kh_ref, key_sems), (value_ref, vh_ref, value_sems))
+        (
+            (query_ref, qh_ref, query_sems), (key_ref, kh_ref, key_sems),
+            (value_ref, vh_ref, value_sems), (grad_ref, gh_ref, grad_sems),
+        )
     ):
         split_rows(matrix_ref, rows_ref, sorted_ref, send_ref.at[index])
         sends.append(
@@ -159,13 +181,12 @@
                 sums_ref[my_group, index, place : place + 1, :] = row_sums(squares[place * PER : (place + 1) * PER])
         if index == 1:
             sums_sends = send_all("head", lambda peer: sums_ref.at[my_group], sums_ref.at[my_group], sums_sems)
-    receive_all(sums_sends)
-    total = sums_ref[0]
-    for group in range(1, sums_ref.shape[0]):
-        total = total + sums_ref[group]
-    inverse_ref[me] = lax.rsqrt(total / D + EPSILON)
-    inverse_sends = send_all("ctx", lambda peer: inverse_ref.at[me], inverse_ref.at[me], inverse_sems)
-    split_rows(matrix_ref, grad_ref, sorted_ref, grad_heads_ref)
+            receive_all(sums_sends)
+            total = sums_ref[0]
+            for group in range(1, sums_ref.shape[0]):
+                total = total + sums_ref[group]
+            inverse_ref[me] = lax.rsqrt(total / D + EPSILON)
+            inverse_sends = send_all("ctx", lambda peer: inverse_ref.at[me], inverse_ref.at[me], inverse_sems)
     receive_all(inverse_sends)
     for index, (arrived_ref, gain_ref, normed_ref) in enumerate(
         ((qh_ref, query_gain_ref, qn_ref), (kh_ref, key_gain_ref, kn_ref))
@@ -174,14 +195,26 @@
 
         def normalise(seg, carry):
             for place in range(CLASSES):
-                rows = slice(place * PER, (place + 1) * PER)
                 inverse = inverse_ref[seg, index, pl.ds((residue + ORDER[place]) % CLASSES, 1), :]
-                normed = arrived_ref[seg, rows, :].astype(jnp.float32) * columns(inverse) * gain_ref[...]
-                normed_ref[seg, rows, :] = normed.astype(jnp.bfloat16)
+                normed = arrived_ref[seg, place].astype(jnp.float32) * columns(inverse) * gain_ref[...]
+                normed_ref[seg, place] = normed.astype(jnp.bfloat16)
+                if index == 1:
+                    store_block_rows(kb_ref, seg, place, normed.astype(jnp.bfloat16))
             return carry
 
         lax.fori_loop(0, segs, normalise, 0)
     receive_all(sends[2])
+
+    def value_blocks(seg, carry):
+        for place in range(CLASSES):
+            store_block_rows(vb_ref, seg, place, vh_ref[seg, place])
+        return carry
+
+    lax.fori_loop(0, segs, value_blocks, 0)
+    forward_pass(
+        slots, blocks_ref, qn_ref, kn_ref, vh_ref, kb_ref, vb_ref, out_ref, merged_ref, lse_ref, max_ref, total_ref
+    )
+    receive_all(sends[3])
     for copies in sends + [sums_sends, inverse_sends]:
         finish_sends(copies)
 
@@ -197,7 +230,10 @@
     residue = head_residue(heads_local)
     pairs = ((qh_ref, dq_ref, query_gain_ref), (kh_ref, dk_ref, key_gain_ref))
     meet_peers()
-    sends = [send_all("ctx", lambda peer: dv_ref.at[peer], arrived_ref.at[2, me], value_sems)]
+    half = SEG // 2
+    first_sends = send_all(
+        "ctx", lambda peer: dv_ref.at[peer, :half], arrived_ref.at[2, me, :half], value_sems.at[0]
+    )
     arrived_ref[2, me] = dv_ref[me]
 
     def inner_products(seg, carry):
@@ -210,6 +246,10 @@
 
     lax.fori_loop(0, segs, inner_products, 0)
     inner_sends = send_all("ctx", lambda peer: inner_ref.at[peer], inner_in_ref.at[me], inner_sems)
+    second_sends = send_all(
+        "ctx", lambda peer: dv_ref.at[peer, half:], arrived_ref.at[2, me, half:], value_sems.at[1]
+    )
+    sends = [first_sends + second_sends]
     inner_in_ref[me] = inner_ref[me]
     receive_all(inner_sends)
     subtotal = inner_in_ref[0]
@@ -311,8 +351,8 @@
     return joint, total, summed
 
 
-def forward_kernel(
-    slots, blocks_ref, qn_ref, kn_ref, value_ref, out_ref, merged_ref, lse_ref, max_ref, total_ref,
+def forward_pass(
+    slots, blocks_ref, qn_ref, kn_ref, value_ref, kb_ref, vb_ref, out_ref, merged_ref, lse_ref, max_ref, total_ref,
 ):
     segs = qn_ref.shape[0]
 
@@ -322,8 +362,8 @@
         listed = [blocks_ref[seg, slot] for slot in range(slots)]
         memory = part_forward(
             query_rows,
-            jnp.concatenate([take_block(kn_ref, block) for block in listed], axis=0),
-            jnp.concatenate([take_block(value_ref, block) for block in listed], axis=0),
+            jnp.concatenate([kb_ref[block] for block in listed], axis=0),
+            jnp.concatenate([vb_ref[block] for block in listed], axis=0),
         )
         max_ref[seg], total_ref[seg], merged_ref[seg] = merge_parts([own, memory])
         return carry
@@ -497,24 +537,24 @@
     shape = jax.ShapeDtypeStruct
     ctx_sems, head_sems = pltpu.SemaphoreType.DMA((2, segs)), pltpu.SemaphoreType.DMA((2, groups))
     pairs = segs * SEG * SEG * 4
-    query_normed, key_normed, query_heads, key_heads, value_heads, grad_heads, inverse = vmem_call(
-        inbound_kernel,
-        (shape(flat, jnp.bfloat16),) * 5
-        + (shape((heads_local, SEG, DH), jnp.bfloat16), shape((segs,) + sums, jnp.float32)),
+    classed_bf16 = shape(classed, jnp.bfloat16)
+    query_normed, key_normed, query_heads, key_heads, value_heads, grad_heads, inverse, attended, merged, lse = vmem_call(
+        functools.partial(inbound_kernel, slots),
+        (classed_bf16,) * 6
+        + (
+            shape((segs,) + sums, jnp.float32), shape(flat, jnp.bfloat16),
+            shape((segs, DH, SEG), jnp.float32), shape((segs, 1, SEG), jnp.float32),
+        ),
         [
-            pltpu.VMEM((SEG, width), jnp.bfloat16), pltpu.VMEM((3, heads_local, SEG, DH), jnp.bfloat16),
-            pltpu.VMEM((groups,) + sums, jnp.float32), ctx_sems, ctx_sems, ctx_sems, head_sems, ctx_sems,
+            pltpu.VMEM((SEG, width), jnp.bfloat16), pltpu.VMEM((4, heads_local, CLASSES, PER, DH), jnp.bfloat16),
+            pltpu.VMEM((groups,) + sums, jnp.float32),
+            pltpu.VMEM((segs * (SEG // BLOCK), BLOCK, DH), jnp.bfloat16),
+            pltpu.VMEM((segs * (SEG // BLOCK), BLOCK, DH), jnp.bfloat16),
+            pltpu.VMEM((segs, 1, SEG), jnp.float32), pltpu.VMEM((segs, 1, SEG), jnp.float32),
+            ctx_sems, ctx_sems, ctx_sems, ctx_sems, head_sems, ctx_sems,
         ],
-        operand_count=7, flops=8 * SEG * SEG * width, collective_id=0,
-    )(matrix, queries, key_states, values, cotangent, *gains)
-    grad_heads = exchange(jnp.concatenate([grad_heads] * (segs // heads_local), axis=0))
-    query_normed, key_normed = query_normed.reshape(classed), key_normed.reshape(classed)
-    attended, merged, lse = vmem_call(
-        functools.partial(forward_kernel, slots),
-        (shape(flat, jnp.bfloat16), shape((segs, DH, SEG), jnp.float32), shape((segs, 1, SEG), jnp.float32)),
-        [pltpu.VMEM((segs, 1, SEG), jnp.float32)] * 2,
-        operand_count=4, smem_first=True, flops=pairs * DH * 4,
-    )(memory_blocks, query_normed, key_normed, value_heads.reshape(classed))
+        operand_count=8, smem_first=True, flops=pairs * DH * 4, collective_id=0,
+    )(memory_blocks, matrix, queries, key_states, values, cotangent, *gains)
     attended = exchange(attended)
     dq, dk, dv = vmem_call(
         functools.partial(backward_kernel, slots),
@@ -525,7 +565,7 @@
         ],
         operand_count=7, smem_first=True, flops=pairs * DH * 10,
     )(
-        memory_blocks, query_normed, key_normed, value_heads.reshape(classed), grad_heads.reshape(classed),
+        memory_blocks, query_normed, key_normed, value_heads, grad_heads,
         merged, lse,
     )
     return vmem_call(
@@ -536,10 +576,10 @@
             pltpu.VMEM((3,) + flat, jnp.bfloat16), pltpu.VMEM((segs,) + sums, jnp.float32),
             pltpu.VMEM((segs,) + sums, jnp.float32), pltpu.VMEM((groups,) + sums, jnp.float32),
             pltpu.VMEM((segs,) + sums, jnp.float32),
-            ctx_sems, ctx_sems, ctx_sems, ctx_sems, head_sems, ctx_sems,
+            ctx_sems, ctx_sems, pltpu.SemaphoreType.DMA((2, 2, segs)), ctx_sems, head_sems, ctx_sems,
         ],
         operand_count=10, flops=8 * SEG * SEG * width, collective_id=1,
-    )(matrix, attended, dv, dq, dk.reshape(flat), query_heads, key_heads, inverse, *gains)
+    )(matrix, attended, dv, dq, dk.reshape(flat), query_heads.reshape(flat), key_heads.reshape(flat), inverse, *gains)
 
 
 def solution(mesh):

time: 252 us -> 250 us (level); the launches traced: 247 us -> 250 us
  Pallas kernels: 229 us -> 238 us
  starting transfers between devices: 8.46 us -> 3.87 us
    pallas_call x2 -> x1, Pallas kernels: 109 us -> 115 us  [head_shards(): vmem_call(functools.partial(inbound_kernel, slots), (classed_bf16,) * 6 +...]
    all_to_all x2 -> x1, starting transfers between devices: 8.46 us -> 3.87 us  [exchange(): return lax.all_to_all(heads, 'ctx', split_axis=0, concat_axis=0, tiled=True)]
    unnamed x14 -> x12, local copies, waits for them, and re-layouts: 6.3 us -> 6.3 us
  transfers between devices with their start and end apart: 2 -> 1, of which waited for: 1 -> 0; matrix products, arithmetic and copies ran while one was open for 0% -> 0% of each run, Pallas kernels for 23% -> 14%
where the time goes in v3:
time: 250 us
  Pallas kernels  238 us (95%)
  local copies, waits for them, and re-layouts  6.3 us (3%)
  starting transfers between devices  3.87 us (2%)
    pallas_call x1, Pallas kernels, head_shards(): vmem_call(functools.partial(inbound_kernel, slots), (classed_bf16,) * 6 +...  115 us
    pallas_call x1, Pallas kernels, head_shards(): vmem_call(outbound_kernel, (shape((SEG, width), jnp.bfloat16),) * 4, [plt...  88.2 us
    pallas_call x1, Pallas kernels, head_shards(): vmem_call(functools.partial(backward_kernel, slots), (shape(flat, jnp.flo...  33.9 us
    unnamed x12, local copies, waits for them, and re-layouts  6.3 us
  transfers between devices with their start and end apart: 1, of which 0 were waited for; matrix products, arithmetic and copies ran while one was open for 0% of the time, Pallas kernels for 14%

profile of v3, /device:TPU:0, one launch (start us, length us, event | category | flops | bytes accessed | tf_op | source)
XLA Modules:
  0.0 249.7 jit_solution(5138444232626199000)
XLA Ops:
  0.6 1.3 bitcast_convert_fusion
  1.9 115.5 %shard_map.111 = (bf16[8,8,64,128]{3,2,1,0:T(8,128)(2,1)}, bf16[8,8,64,128]{3,2,1,0:T(8,128)(2,1)}, bf16[8,8,64,128]{3,2,1,0:T(8,128)(2,1)}, bf16[8,8,64,128]{3,...) custom-call(s32[8,8]{1,0:T(8,128)} %blocks_ref.3, ...), custom_call_target="tpu_custom_call" | custom-call | flops 4294967296 | bytes 8388608 | tf_op jit(solution)/shard_map/pallas_call | solution.py:541
  117.4 3.9 %all-to-all-start = ((bf16[8,512,128]{2,1,0:T(8,128)(2,1)}), bf16[8,512,128]{2,1,0:T(8,128)(2,1)S(1)}, u32[]{:S(2)}, u32[]{:S(2)}) async-start(bf16[8,512,128]{2,1,0:T(8,128)(2,1)} %get-tuple-element.17), calls=%async_computation | async-start | bytes 2097152 | tf_op jit(solution)/shard_map/all_to_all | solution.py:520
  121.3 33.9 %shard_map.112 = (f32[8,512,128]{2,1,0:T(8,128)}, f32[8,8,64,128]{3,2,1,0:T(8,128)}, bf16[8,512,128]{2,1,0:T(8,128)(2,1)}) custom-call(s32[8,8]{1,0:T(8,128)} %blocks_ref.3, bf16[8,8,64,128]{3,2,1,0:T(8,128)(2,1)} %get-tuple-element.18.qn_ref, bf16[8,8,64,128]{3,2,1,0:T(8,128)(2,1)} %get-tuple-element.19.kn_ref, ...), custom_call_target="tpu_custom_call" | custom-call | flops 10737418240 | bytes 8388608 | tf_op jit(solution)/shard_map/pallas_call | solution.py:559
  155.2 0.0 all-to-all-done.attended_ref
  155.2 0.0 copy-start
  155.2 1.0 copy-done
  156.1 88.2 %shard_map.113 = (bf16[512,1024]{1,0:T(8,128)(2,1)}, bf16[512,1024]{1,0:T(8,128)(2,1)}, bf16[512,1024]{1,0:T(8,128)(2,1)}, bf16[512,1024]{1,0:T(8,128)(2,1)}) custom-call(bf16[512,512]{1,0:T(8,128)(2,1)} %constant.26.clone.matrix_ref, bf16[8,512,128]{2,1,0:T(8,128)(2,1)} %copy-done, bf16[8,512,128]{2,1,0:T(8,128)(2,1)} %get-tuple-element.24.dv_ref, ...), custom_call_target="tpu_custom_call" | custom-call | flops 2147483648 | bytes 8388608 | tf_op jit(solution)/shard_map/pallas_call | solution.py:571
  244.3 0.0 copy-start.3
  244.4 0.0 copy-start.2
  244.4 2.4 copy.16
  246.8 0.0 copy-done.3
  246.8 0.0 copy-start.1
  246.8 1.0 copy.17
  247.7 0.0 copy-done.2
  247.8 1.0 copy.18
  248.7 0.0 copy-done.1
  248.7 1.0 copy.19
Async XLA Ops:
  117.4 37.7 %all-to-all-start = ((bf16[8,512,128]{2,1,0:T(8,128)(2,1)}), bf16[8,512,128]{2,1,0:T(8,128)(2,1)S(1)}, u32[]{:S(2)}, u32[]{:S(2)}) async-start(bf16[8,512,128]{2,1,0:T(8,128)(2,1)} %get-tuple-element.17), calls=%async_computation | async-start | bytes 2097152 | tf_op jit(solution)/shard_map/all_to_all | solution.py:520
  155.2 1.0 copy-start
  244.3 2.4 copy-start.3
  244.4 3.4 %copy-start.2 = (bf16[512,1024]{1,0:T(8,128)(2,1)S(1)}, bf16[512,1024]{1,0:T(8,128)(2,1)}, u32[]{:S(2)}) copy-start(bf16[512,1024]{1,0:T(8,128)(2,1)} %get-tuple-element.38) | copy-start | bytes 3145732
  246.8 1.9 copy-start.1

commit v4 on v3

--- a/solution.py
+++ b/solution.py
@@ -220,9 +220,10 @@
 
 
 def outbound_kernel(
-    matrix_ref, attended_ref, dv_ref, dq_ref, dk_ref, qh_ref, kh_ref, inverse_ref, query_gain_ref, key_gain_ref,
+    matrix_ref, attended_ref, dqt_in_ref, dk_in_ref, dv_in_ref, qn_ref, kn_ref, value_ref, cotangent_ref, lse_ref,
+    delta_ref, qh_ref, kh_ref, inverse_ref, query_gain_ref, key_gain_ref,
     out_ref, query_grads_ref, key_grads_ref, value_grads_ref,
-    sorted_ref, send_ref, arrived_ref, inner_ref, inner_in_ref, group_ref, total_ref,
+    dq_ref, dk_ref, dv_ref, sorted_ref, send_ref, arrived_ref, inner_ref, inner_in_ref, group_ref, total_ref,
     query_sems, key_sems, value_sems, inner_sems, group_sems, total_sems,
 ):
     segs, heads_local = dv_ref.shape[0], out_ref.shape[1] // DH
@@ -231,9 +232,21 @@
     pairs = ((qh_ref, dq_ref, query_gain_ref), (kh_ref, dk_ref, key_gain_ref))
     meet_peers()
     half = SEG // 2
-    first_sends = send_all(
-        "ctx", lambda peer: dv_ref.at[peer, :half], arrived_ref.at[2, me, :half], value_sems.at[0]
-    )
+
+    def own_level(seg):
+        dqt, dk, dv = part_backward(
+            qn_ref[seg], kn_ref[seg], value_ref[seg], cotangent_ref[seg], lse_ref[seg], delta_ref[seg]
+        )
+        dv_ref[seg] = (dv_in_ref[seg] + dv).astype(jnp.bfloat16)
+        dk_ref[seg] = dk_in_ref[seg] + dk
+        dq_ref[seg] = (dqt_in_ref[seg] + dqt).T
+
+    def finished_values(seg):
+        own_level(seg)
+        return dv_ref.at[seg, :half]
+
+    first_sends = send_all("ctx", finished_values, arrived_ref.at[2, me, :half], value_sems.at[0])
+    own_level(me)
     arrived_ref[2, me] = dv_ref[me]
 
     def inner_products(seg, carry):
@@ -429,22 +442,21 @@
 
 def backward_kernel(
     slots, blocks_ref, qn_ref, kn_ref, value_ref, grad_ref, merged_ref, lse_ref,
-    dq_ref, dk_ref, dv_ref, delta_ref, dqt_ref, dvf_ref,
+    dqt_ref, dk_ref, dvf_ref, delta_ref,
 ):
     segs = qn_ref.shape[0]
     own_refs = (qn_ref, kn_ref, value_ref, grad_ref)
 
-    def own_level(seg, carry):
+    def start(seg, carry):
         grad_float = grad_ref[seg].reshape(SEG, DH).astype(jnp.float32)
         delta = jnp.sum(grad_float.T * merged_ref[seg], axis=0, keepdims=True)
         delta_ref[seg] = delta
-        dqt, dk, dv = part_backward(*(take_rows(ref, [seg], CLASSES) for ref in own_refs), lse_ref[seg], delta)
-        dqt_ref[seg] = dqt
-        dk_ref[seg] = dk.reshape(CLASSES, PER, DH)
-        dvf_ref[seg] = dv.reshape(CLASSES, PER, DH)
-        return carry
-
-    lax.fori_loop(0, segs, own_level, 0)
+        dqt_ref[seg] = jnp.zeros(dqt_ref.shape[1:], jnp.float32)
+        dk_ref[seg] = jnp.zeros(dk_ref.shape[1:], jnp.float32)
+        dvf_ref[seg] = jnp.zeros(dvf_ref.shape[1:], jnp.float32)
+        return carry
+
+    lax.fori_loop(0, segs, start, 0)
 
     def memory(seg, carry):
         query_rows = take_rows(qn_ref, [seg], CLASSES)
@@ -507,13 +519,6 @@
         return carry
 
     lax.fori_loop(0, segs // 4, upper_levels, 0)
-
-    def finish(seg, carry):
-        dq_ref[seg] = dqt_ref[seg].T
-        dv_ref[seg] = dvf_ref[seg].reshape(SEG, DH).astype(jnp.bfloat16)
-        return carry
-
-    lax.fori_loop(0, segs, finish, 0)
 
 
 def exchange(heads):
@@ -556,30 +561,31 @@
         operand_count=8, smem_first=True, flops=pairs * DH * 4, collective_id=0,
     )(memory_blocks, matrix, queries, key_states, values, cotangent, *gains)
     attended = exchange(attended)
-    dq, dk, dv = vmem_call(
+    dqt, dk, dv, delta = vmem_call(
         functools.partial(backward_kernel, slots),
-        (shape(flat, jnp.float32), shape(classed, jnp.float32), shape(flat, jnp.bfloat16)),
-        [
-            pltpu.VMEM((segs, 1, SEG), jnp.float32), pltpu.VMEM((segs, DH, SEG), jnp.float32),
-            pltpu.VMEM(classed, jnp.float32),
-        ],
+        (
+            shape((segs, DH, SEG), jnp.float32), shape(classed, jnp.float32), shape(classed, jnp.float32),
+            shape((segs, 1, SEG), jnp.float32),
+        ),
         operand_count=7, smem_first=True, flops=pairs * DH * 10,
-    )(
-        memory_blocks, query_normed, key_normed, value_heads, grad_heads,
-        merged, lse,
-    )
+    )(memory_blocks, query_normed, key_normed, value_heads, grad_heads, merged, lse)
+    own = [array.reshape(flat) for array in (query_normed, key_normed, value_heads, grad_heads)]
     return vmem_call(
         outbound_kernel,
         (shape((SEG, width), jnp.bfloat16),) * 4,
         [
+            pltpu.VMEM(flat, jnp.float32), pltpu.VMEM(flat, jnp.float32), pltpu.VMEM(flat, jnp.bfloat16),
             pltpu.VMEM((SEG, width), jnp.bfloat16), pltpu.VMEM((2,) + flat, jnp.bfloat16),
             pltpu.VMEM((3,) + flat, jnp.bfloat16), pltpu.VMEM((segs,) + sums, jnp.float32),
             pltpu.VMEM((segs,) + sums, jnp.float32), pltpu.VMEM((groups,) + sums, jnp.float32),
             pltpu.VMEM((segs,) + sums, jnp.float32),
             ctx_sems, ctx_sems, pltpu.SemaphoreType.DMA((2, 2, segs)), ctx_sems, head_sems, ctx_sems,
         ],
-        operand_count=10, flops=8 * SEG * SEG * width, collective_id=1,
-    )(matrix, attended, dv, dq, dk.reshape(flat), query_heads.reshape(flat), key_heads.reshape(flat), inverse, *gains)
+        operand_count=16, flops=8 * SEG * SEG * width, collective_id=1,
+    )(
+        matrix, attended, dqt, dk.reshape(flat), dv.reshape(flat), *own, lse, delta,
+        query_heads.reshape(flat), key_heads.reshape(flat), inverse, *gains,
+    )
 
 
 def solution(mesh):

time: 250 us -> 245 us (0.980)
  Pallas kernels: 238 us -> 233 us
    pallas_call x1, Pallas kernels: 33.9 us -> 26.8 us  [head_shards(): vmem_call(functools.partial(backward_kernel, slots), (shape((segs, DH, SE...]
  transfers between devices with their start and end apart: 1 -> 1, of which waited for: 0 -> 0; matrix products, arithmetic and copies ran while one was open for 0% -> 0% of each run, Pallas kernels for 14% -> 11%
where the time goes in v4:
time: 245 us
  Pallas kernels  233 us (95%)
  local copies, waits for them, and re-layouts  6.3 us (3%)
  starting transfers between devices  3.87 us (2%)
    pallas_call x1, Pallas kernels, head_shards(): vmem_call(functools.partial(inbound_kernel, slots), (classed_bf16,) * 6 +...  115 us
    pallas_call x1, Pallas kernels, head_shards(): vmem_call(outbound_kernel, (shape((SEG, width), jnp.bfloat16),) * 4, [plt...  90.3 us
    pallas_call x1, Pallas kernels, head_shards(): vmem_call(functools.partial(backward_kernel, slots), (shape((segs, DH, SE...  26.8 us
    unnamed x12, local copies, waits for them, and re-layouts  6.3 us
  transfers between devices with their start and end apart: 1, of which 0 were waited for; matrix products, arithmetic and copies ran while one was open for 0% of the time, Pallas kernels for 11%

profile of v4, /device:TPU:0, one launch (start us, length us, event | category | flops | bytes accessed | tf_op | source)
XLA Modules:
  0.0 244.7 jit_solution(17559118397158571388)
XLA Ops:
  0.6 1.3 bitcast_convert_fusion
  1.9 115.5 %shard_map.111 = (bf16[8,8,64,128]{3,2,1,0:T(8,128)(2,1)}, bf16[8,8,64,128]{3,2,1,0:T(8,128)(2,1)}, bf16[8,8,64,128]{3,2,1,0:T(8,128)(2,1)}, bf16[8,8,64,128]{3,...) custom-call(s32[8,8]{1,0:T(8,128)} %blocks_ref.3, ...), custom_call_target="tpu_custom_call" | custom-call | flops 4294967296 | bytes 8388608 | tf_op jit(solution)/shard_map/pallas_call | solution.py:546
  117.4 3.9 %all-to-all-start = ((bf16[8,512,128]{2,1,0:T(8,128)(2,1)}), bf16[8,512,128]{2,1,0:T(8,128)(2,1)S(1)}, u32[]{:S(2)}, u32[]{:S(2)}) async-start(bf16[8,512,128]{2,1,0:T(8,128)(2,1)} %get-tuple-element.18), calls=%async_computation | async-start | bytes 2097152 | tf_op jit(solution)/shard_map/all_to_all | solution.py:525
  121.3 26.8 %shard_map.112 = (f32[8,128,512]{2,1,0:T(8,128)}, f32[8,8,64,128]{3,2,1,0:T(8,128)}, f32[8,8,64,128]{3,2,1,0:T(8,128)}, f32[8,1,512]{2,1,0:T(1,128)}) custom-call(s32[8,8]{1,0:T(8,128)} %blocks_ref.3, bf16[8,8,64,128]{3,2,1,0:T(8,128)(2,1)} %get-tuple-element.19.qn_ref, bf16[8,8,64,128]{3,2,1,0:T(8,128)(2,1)} %get-tuple-element.20.kn_ref, ...), custom_call_target="tpu_custom_call" | custom-call | flops 10737418240 | bytes 8388608 | tf_op jit(solution)/shard_map/pallas_call | solution.py:564
  148.1 0.0 all-to-all-done.attended_ref
  148.1 0.0 copy-start
  148.1 1.0 copy-done
  149.0 90.3 %shard_map.113 = (bf16[512,1024]{1,0:T(8,128)(2,1)}, bf16[512,1024]{1,0:T(8,128)(2,1)}, bf16[512,1024]{1,0:T(8,128)(2,1)}, bf16[512,1024]{1,0:T(8,128)(2,1)}) custom-call(bf16[512,512]{1,0:T(8,128)(2,1)} %constant.26.clone.matrix_ref, bf16[8,512,128]{2,1,0:T(8,128)(2,1)} %copy-done, f32[8,128,512]{2,1,0:T(8,128)} %get-tuple-element.25.dqt_in_ref, ...), custom_call_target="tpu_custom_call" | custom-call | flops 2147483648 | bytes 8388608 | tf_op jit(solution)/shard_map/pallas_call | solution.py:573
  239.4 0.0 copy-start.3
  239.4 0.0 copy-start.2
  239.4 2.4 copy.16
  241.8 0.0 copy-done.3
  241.8 0.0 copy-start.1
  241.8 1.0 copy.17
  242.8 0.0 copy-done.2
  242.8 1.0 copy.18
  243.7 0.0 copy-done.1
  243.7 1.0 copy.19
Async XLA Ops:
  117.4 30.7 %all-to-all-start = ((bf16[8,512,128]{2,1,0:T(8,128)(2,1)}), bf16[8,512,128]{2,1,0:T(8,128)(2,1)S(1)}, u32[]{:S(2)}, u32[]{:S(2)}) async-start(bf16[8,512,128]{2,1,0:T(8,128)(2,1)} %get-tuple-element.18), calls=%async_computation | async-start | bytes 2097152 | tf_op jit(solution)/shard_map/all_to_all | solution.py:525
  148.1 1.0 copy-start
  239.4 2.4 copy-start.3
  239.4 3.4 %copy-start.2 = (bf16[512,1024]{1,0:T(8,128)(2,1)S(1)}, bf16[512,1024]{1,0:T(8,128)(2,1)}, u32[]{:S(2)}) copy-start(bf16[512,1024]{1,0:T(8,128)(2,1)} %get-tuple-element.40) | copy-start | bytes 3145732
  241.8 1.9 copy-start.1
